TPU v7x, 32 devices: a whole 2x2x4 slice. The times are simulated.
32 devices in a mesh: group: 2 (over y), seq: 8 (over z, x), head: 2 (over core).
Axes of the slice: x: 2, y: 2, z: 4, core: 2. Of those that a mesh axis runs over, the one named last changes fastest.
Arguments:
- response_query: bfloat16 [16, 128, 4096], P('group', 'seq', 'head'), parts along dimension 0, may hold values from -6 to 6, as said below
- response_key: bfloat16 [16, 128, 512], P('group', 'seq', 'head'), parts along dimension 0, may hold values from -8 to 8, as said below
- response_value: bfloat16 [16, 128, 512], P('group', 'seq', 'head'), parts along dimension 0, may hold values from -6 to 6
- response_grad: bfloat16 [16, 128, 4096], P('group', 'seq', 'head'), parts along dimension 0, may hold values from -6 to 6
- prompt_key: bfloat16 [192, 512], P(('group', 'seq'), 'head'), parts along dimension 0, may hold values from -8 to 8, as said below
- prompt_value: bfloat16 [192, 512], P(('group', 'seq'), 'head'), parts along dimension 0, may hold values from -6 to 6
- lengths: int32 [16], P('group'), parts along dimension 0, may hold values from 1 to 128, 512 in all
- home_rank: int32 [16], P('group'), parts along dimension 0, may hold values from 0 to 7, each once
- prompt_seen: int32 [16], P('group'), parts along dimension 0, may hold values from 24 to 96
Outputs:
- response_output: bfloat16 [16, 128, 4096], P(('group', 'seq'), None, 'head'), parts along dimension 0
- response_query_grad: bfloat16 [16, 128, 4096], P('group', 'seq', 'head'), parts along dimension 0
- response_key_grad: bfloat16 [16, 128, 512], P('group', 'seq', 'head'), parts along dimension 0
- response_value_grad: bfloat16 [16, 128, 512], P('group', 'seq', 'head'), parts along dimension 0
- prompt_key_grad: bfloat16 [192, 512], P(('group', 'seq'), 'head'), parts along dimension 0
- prompt_value_grad: bfloat16 [192, 512], P(('group', 'seq'), 'head'), parts along dimension 0
There are 2 independent parts, one for each index of `group`. A program takes and returns all parts, laid end to end along the dimension named above; each array names one. Nothing has to cross between parts.
Inputs may be any that keep to these rules, and one draw needn't show every extreme that they name: `response_query`: queries are finite. `response_key`: keys are finite. `prompt_key`: keys are finite. `lengths`: some response has exactly 128 tokens. `home_rank`: every index of seq is the home of exactly one response.
All inputs are finite; a program needn't handle non-finite values.
Results may differ from a plain program's by a relative error of at most 0.017.
The roundings to bfloat16 on the way count: a program that leaves them out, or rounds other values in their place, can miss the bound.
Values may be sent and summed in bfloat16 or wider, within the bound.
A program may use at most 128 MiB of HBM per device.

v0:
```python
import jax
import jax.numpy as jnp
from jax import lax
from jax.sharding import PartitionSpec as P

HEAD_DIM = 128


NEG_FILL = -1e30


def head_logits(queries, all_keys, allowed, head_index, group_size, scale_factor):
    row_count = queries.shape[0]
    low = head_index * group_size * HEAD_DIM
    high = (head_index + 1) * group_size * HEAD_DIM
    query_head = queries[:, low:high].reshape(row_count, group_size, HEAD_DIM)
    key_head = all_keys[:, head_index * HEAD_DIM : (head_index + 1) * HEAD_DIM]
    logits = (
        jnp.einsum("rhd,kd->rhk", query_head, key_head, preferred_element_type=jnp.float32)
        * scale_factor
    )
    return (query_head, key_head, jnp.where(allowed[:, None, :], logits, NEG_FILL))


def forward(queries, all_keys, all_values, allowed, live_rows, scale_factor):
    row_count = queries.shape[0]
    kv_count = all_keys.shape[1] // HEAD_DIM
    group_size = queries.shape[1] // all_keys.shape[1]
    outputs = []
    totals = []
    for head_index in range(kv_count):
        query_head, key_head, logits = head_logits(
            queries, all_keys, allowed, head_index, group_size, scale_factor
        )
        value_head = all_values[:, head_index * HEAD_DIM : (head_index + 1) * HEAD_DIM]
        row_max = jnp.max(logits, axis=2, keepdims=True)
        log_total = row_max + jnp.log(jnp.sum(jnp.exp(logits - row_max), axis=2, keepdims=True))
        weights = jnp.exp(logits - log_total).astype(jnp.bfloat16)
        mixed = jnp.einsum("rhk,kd->rhd", weights, value_head, preferred_element_type=jnp.float32)
        output_head = jnp.where(live_rows[:, None, None], mixed, 0.0).astype(jnp.bfloat16)
        outputs.append(output_head.reshape(row_count, group_size * HEAD_DIM))
        totals.append(log_total)
    return (jnp.concatenate(outputs, axis=1), totals)


def head_terms(grad_rows, live_rows, output, head_index, group_size):
    row_count = grad_rows.shape[0]
    low = head_index * group_size * HEAD_DIM
    high = (head_index + 1) * group_size * HEAD_DIM
    grad_head = jnp.where(live_rows[:, None], grad_rows[:, low:high], jnp.zeros((), jnp.bfloat16))
    grad_head = grad_head.reshape(row_count, group_size, HEAD_DIM)
    output_head = lax.optimization_barrier(output[:, low:high]).reshape(
        row_count, group_size, HEAD_DIM
    )
    row_dot = jnp.sum(
        grad_head.astype(jnp.float32) * output_head.astype(jnp.float32), axis=2, keepdims=True
    )
    return (grad_head, row_dot)


def backward(
    queries, all_keys, all_values, grad_rows, allowed, live_rows, output, totals, scale_factor
):
    row_count = queries.shape[0]
    kv_count = all_keys.shape[1] // HEAD_DIM
    group_size = queries.shape[1] // all_keys.shape[1]
    query_grads = []
    key_grads = []
    value_grads = []
    for head_index in range(kv_count):
        query_head, key_head, logits = head_logits(
            queries, all_keys, allowed, head_index, group_size, scale_factor
        )
        value_head = all_values[:, head_index * HEAD_DIM : (head_index + 1) * HEAD_DIM]
        prob = jnp.exp(logits - totals[head_index])
        weights = prob.astype(jnp.bfloat16)
        grad_head, row_dot = head_terms(grad_rows, live_rows, output, head_index, group_size)
        spread = jnp.einsum(
            "rhd,kd->rhk", grad_head, value_head, preferred_element_type=jnp.float32
        )
        dlogit = (prob * (spread - row_dot)).astype(jnp.bfloat16)
        query_part = (
            jnp.einsum("rhk,kd->rhd", dlogit, key_head, preferred_element_type=jnp.float32)
            * scale_factor
        )
        query_grads.append(query_part.reshape(row_count, group_size * HEAD_DIM))
        key_grads.append(
            jnp.einsum("rhk,rhd->kd", dlogit, query_head, preferred_element_type=jnp.float32)
            * scale_factor
        )
        value_grads.append(
            jnp.einsum("rhk,rhd->kd", weights, grad_head, preferred_element_type=jnp.float32)
        )
    return (
        jnp.concatenate(query_grads, axis=1),
        jnp.concatenate(key_grads, axis=1),
        jnp.concatenate(value_grads, axis=1),
    )


def body(
    response_query,
    response_key,
    response_value,
    response_grad,
    prompt_key,
    prompt_value,
    lengths,
    home_rank,
    prompt_seen,
):
    rank_count = home_rank.shape[0]
    rank_ids = jnp.arange(rank_count, dtype=jnp.int32)
    resident = jnp.sum(
        jnp.where(home_rank[None, :] == rank_ids[:, None], rank_ids[None, :], 0), axis=1
    )
    own_rank = lax.axis_index("seq")
    scale_factor = 1.0 / HEAD_DIM**0.5
    arrived = (
        lax.all_to_all(response_query[resident], "seq", split_axis=0, concat_axis=1, tiled=True),
        lax.all_to_all(response_key[resident], "seq", split_axis=0, concat_axis=1, tiled=True),
        lax.all_to_all(response_value[resident], "seq", split_axis=0, concat_axis=1, tiled=True),
        lax.all_to_all(response_grad[resident], "seq", split_axis=0, concat_axis=1, tiled=True),
    )
    queries = arrived[0][0]
    own_keys = arrived[1][0]
    own_values = arrived[2][0]
    grad_rows = arrived[3][0]
    own_response = resident[own_rank]
    length = lengths[own_response]
    visible = prompt_seen[own_response]
    max_length = queries.shape[0]
    prompt_rows = prompt_key.shape[0]
    prompt_total = prompt_rows * lax.axis_size("seq")
    positions = jnp.arange(max_length, dtype=jnp.int32)
    prompt_cols = jnp.arange(prompt_total, dtype=jnp.int32)
    seen_part = jnp.broadcast_to(prompt_cols[None, :] < visible, (max_length, prompt_total))
    allowed = jnp.concatenate([seen_part, positions[None, :] <= positions[:, None]], axis=1)
    live_rows = positions < length
    gathered_keys, gathered_values = (
        lax.all_gather(prompt_key, "seq", axis=0, tiled=True),
        lax.all_gather(prompt_value, "seq", axis=0, tiled=True),
    )
    all_keys = jnp.concatenate([gathered_keys, own_keys], axis=0)
    all_values = jnp.concatenate([gathered_values, own_values], axis=0)
    response_out, response_totals = forward(
        queries, all_keys, all_values, allowed, live_rows, scale_factor
    )
    query_grad, key_grad, value_grad = backward(
        queries,
        all_keys,
        all_values,
        grad_rows,
        allowed,
        live_rows,
        response_out,
        response_totals,
        scale_factor,
    )
    key_summed, value_summed = (
        lax.psum_scatter(key_grad[:prompt_total], "seq", scatter_dimension=0, tiled=True),
        lax.psum_scatter(value_grad[:prompt_total], "seq", scatter_dimension=0, tiled=True),
    )
    returned = (
        lax.all_to_all(
            query_grad.astype(jnp.bfloat16)[None], "seq", split_axis=1, concat_axis=0, tiled=True
        ),
        lax.all_to_all(
            key_grad[prompt_total:].astype(jnp.bfloat16)[None],
            "seq",
            split_axis=1,
            concat_axis=0,
            tiled=True,
        ),
        lax.all_to_all(
            value_grad[prompt_total:].astype(jnp.bfloat16)[None],
            "seq",
            split_axis=1,
            concat_axis=0,
            tiled=True,
        ),
    )
    return (
        response_out[None],
        returned[0][home_rank],
        returned[1][home_rank],
        returned[2][home_rank],
        key_summed.astype(jnp.bfloat16),
        value_summed.astype(jnp.bfloat16),
    )


def solution(mesh):
    placed = (
        P("group", "seq", "head"),
        P("group", "seq", "head"),
        P("group", "seq", "head"),
        P("group", "seq", "head"),
        P(("group", "seq"), "head"),
        P(("group", "seq"), "head"),
        P("group"),
        P("group"),
        P("group"),
    )
    return jax.shard_map(
        body,
        mesh=mesh,
        in_specs=placed,
        out_specs=(
            P(("group", "seq"), None, "head"),
            P("group", "seq", "head"),
            P("group", "seq", "head"),
            P("group", "seq", "head"),
            P(("group", "seq"), "head"),
            P(("group", "seq"), "head"),
        ),
        check_vma=False,
    )
```

profile of v0, /device:TPU:0, one launch (start us, length us, event | category | flops | bytes accessed | tf_op | source)
XLA Modules:
  0.0 196.7 jit_solution(3605869147865452374)
XLA Ops:
  1.7 1.4 gather_fusion.3
  3.1 7.4 %all-to-all-start.3 = ((bf16[8,16,2048]{2,1,0:T(8,128)(2,1)}), bf16[8,16,2048]{2,1,0:T(8,128)(2,1)S(1)}, u32[]{:S(2)}, u32[]{:S(2)}) async-start(bf16[8,16,2048]{2,1,0:T(8,128)(2,1)} %gather_fusion.3), calls=%async_computation.3 | async-start | bytes 1048576 | tf_op jit(solution)/shard_map/all_to_all | solution.py:123
  10.5 1.4 gather_fusion
  11.8 13.1 %all-to-all-done.3 = bf16[8,16,2048]{2,1,0:T(8,128)(2,1)S(1)} async-done(((bf16[8,16,2048]{2,1,0:T(8,128)(2,1)}), bf16[8,16,2048]{2,1,0:T(8,128)(2,1)S(1)}, u32[]{:S(2)}, u32[]{:S(2)}) %all-to-all-start.3) | async-done | bytes 524320 | tf_op jit(solution)/shard_map/all_to_all | solution.py:123
  24.9 3.8 %all-to-all-start = ((bf16[8,16,2048]{2,1,0:T(8,128)(2,1)}), bf16[8,16,2048]{2,1,0:T(8,128)(2,1)S(1)}, u32[]{:S(2)}, u32[]{:S(2)}) async-start(bf16[8,16,2048]{2,1,0:T(8,128)(2,1)} %gather_fusion), calls=%async_computation | async-start | bytes 1048576 | tf_op jit(solution)/shard_map/all_to_all | solution.py:120
  32.5 1.2 gather_fusion.2
  34.9 31.2 %all-gather = bf16[8,12,256]{2,1,0:T(8,128)(2,1)S(1)} all-gather(bf16[1,12,256]{2,1,0:T(8,128)(2,1)S(1)} %bitcast.131), channel_id=1, replica_groups=mesh['group'=2,'seq'=8,'head'=2] {'seq'}, dimensions={0}, use_global_device_ids=true | all-gather | bytes 55296 | tf_op jit(solution)/shard_map/all_gather | solution.py:141
  66.8 30.5 %all-gather.1 = bf16[8,12,256]{2,1,0:T(8,128)(2,1)S(1)} all-gather(bf16[1,12,256]{2,1,0:T(8,128)(2,1)S(1)} %bitcast.132), channel_id=1, replica_groups=mesh['group'=2,'seq'=8,'head'=2] {'seq'}, dimensions={0}, use_global_device_ids=true | all-gather | bytes 55296 | tf_op jit(solution)/shard_map/all_gather | solution.py:142
  100.8 5.2 %all-to-all-start.1 = ((bf16[8,16,256]{2,1,0:T(8,128)(2,1)}), bf16[8,16,256]{2,1,0:T(8,128)(2,1)S(1)}, u32[]{:S(2)}, u32[]{:S(2)}) async-start(bf16[8,16,256]{2,1,0:T(8,128)(2,1)} %gather_fusion.1), calls=%async_computation.1 | async-start | bytes 131072 | tf_op jit(solution)/shard_map/all_to_all | solution.py:121
  106.4 6.5 %all-to-all-done.1 = bf16[8,16,256]{2,1,0:T(8,128)(2,1)S(1)} async-done(((bf16[8,16,256]{2,1,0:T(8,128)(2,1)}), bf16[8,16,256]{2,1,0:T(8,128)(2,1)S(1)}, u32[]{:S(2)}, u32[]{:S(2)}) %all-to-all-start.1) | async-done | bytes 65568 | tf_op jit(solution)/shard_map/all_to_all | solution.py:121
  112.9 3.4 %all-to-all-start.2 = ((bf16[8,16,256]{2,1,0:T(8,128)(2,1)}), bf16[8,16,256]{2,1,0:T(8,128)(2,1)S(1)}, u32[]{:S(2)}, u32[]{:S(2)}) async-start(bf16[8,16,256]{2,1,0:T(8,128)(2,1)} %gather_fusion.2), calls=%async_computation.2 | async-start | bytes 131072 | tf_op jit(solution)/shard_map/all_to_all | solution.py:122
  117.1 6.3 %all-to-all-done.2 = bf16[8,16,256]{2,1,0:T(8,128)(2,1)S(1)} async-done(((bf16[8,16,256]{2,1,0:T(8,128)(2,1)}), bf16[8,16,256]{2,1,0:T(8,128)(2,1)S(1)}, u32[]{:S(2)}, u32[]{:S(2)}) %all-to-all-start.2) | async-done | bytes 65568 | tf_op jit(solution)/shard_map/all_to_all | solution.py:122
  129.0 4.0 %all-to-all-start.6 = ((bf16[8,2,2048]{2,1,0:T(2,128)(2,1)}), bf16[8,2,2048]{2,1,0:T(2,128)(2,1)}, u32[]{:S(2)}, u32[]{:S(2)}) async-start(bf16[8,2,2048]{2,1,0:T(2,128)(2,1)} %reshape.232), calls=%async_computation.6 | async-start | bytes 131072 | tf_op jit(solution)/shard_map/all_to_all | solution.py:175
  136.7 3.2 %all-to-all-done.6 = bf16[8,2,2048]{2,1,0:T(2,128)(2,1)} async-done(((bf16[8,2,2048]{2,1,0:T(2,128)(2,1)}), bf16[8,2,2048]{2,1,0:T(2,128)(2,1)}, u32[]{:S(2)}, u32[]{:S(2)}) %all-to-all-start.6) | async-done | bytes 65568 | tf_op jit(solution)/shard_map/all_to_all | solution.py:175
  139.9 3.4 %all-to-all-start.5 = ((bf16[8,2,2048]{2,1,0:T(2,128)(2,1)}), bf16[8,2,2048]{2,1,0:T(2,128)(2,1)S(1)}, u32[]{:S(2)}, u32[]{:S(2)}) async-start(bf16[8,2,2048]{2,1,0:T(2,128)(2,1)} %reshape.230), calls=%async_computation.5 | async-start | bytes 131072 | tf_op jit(solution)/shard_map/all_to_all | solution.py:168
  144.3 3.7 %reduce = bf16[128,2048]{1,0:T(8,128)(2,1)S(1)} reduce(bf16[128,1,2048]{2,1,0:T(2,128)(2,1)S(1)} %fusion.55, bf16[]{:T(256)} %broadcast.89), dimensions={1}, to_apply=%fusion.55.reduce_sub_computation | reduce | bytes 1048578
  150.1 5.2 %all-to-all-start.4 = ((bf16[8,2,16384]{2,1,0:T(2,128)(2,1)}), bf16[8,2,16384]{2,1,0:T(2,128)(2,1)S(1)}, u32[]{:S(2)}, u32[]{:S(2)}) async-start(bf16[8,2,16384]{2,1,0:T(2,128)(2,1)} %reshape.228), calls=%async_computation.4 | async-start | bytes 1048576 | tf_op jit(solution)/shard_map/all_to_all | solution.py:165
  155.4 23.4 %fusion.51 = (f32[16,256]{1,0:T(8,128)S(1)}, f32[16,256]{1,0:T(8,128)S(1)}) fusion(f32[96,256]{1,0:T(8,128)S(1)} %get-tuple-element.49, f32[96,256]{1,0:T(8,128)S(1)} %get-tuple-element.48), kind=kCustom, calls=%all-reduce-scatter.2 | all-reduce-scatter fusion | flops 65537 | bytes 229888
  178.9 2.0 %collective-permute-start.2 = (bf16[16,256]{1,0:T(8,128)(2,1)S(1)}, bf16[16,256]{1,0:T(8,128)(2,1)S(1)}, u32[]{:S(2)}, u32[]{:S(2)}) collective-permute-start(bf16[16,256]{1,0:T(8,128)(2,1)S(1)} %convert.44), channel_id=1, source_target_pairs={{0,2},{2,4},{4,6},{6,8},{8,10},{10,12},{12,14},{1,3},{3,5},{5,7},{... | collective-permute-start | bytes 24584
  180.9 1.3 collective-permute-start.3
  182.2 3.2 %collective-permute-start = (bf16[16,256]{1,0:T(8,128)(2,1)S(1)}, bf16[16,256]{1,0:T(8,128)(2,1)S(1)}, u32[]{:S(2)}, u32[]{:S(2)}) collective-permute-start(bf16[16,256]{1,0:T(8,128)(2,1)S(1)} %convert.43), channel_id=1, source_target_pairs={{0,2},{2,4},{4,6},{6,8},{8,10},{10,12},{12,14},{1,3},{3,5},{5,7},{... | collective-permute-start | bytes 24584
  185.4 2.8 %collective-permute-start.1 = (bf16[12,256]{1,0:T(8,128)(2,1)S(1)}, bf16[12,256]{1,0:T(8,128)(2,1)S(1)}, u32[]{:S(2)}, u32[]{:S(2)}) collective-permute-start(bf16[12,256]{1,0:T(8,128)(2,1)S(1)} %slice.82), channel_id=1, source_target_pairs={{0,4},{2,6},{4,8},{6,10},{8,12},{10,14},{1,5},{3,7},{5,9},{7,11},{... | collective-permute-start | bytes 18440
  192.1 1.2 gather_fusion.6
  195.3 1.4 gather_fusion.4
  (111 shorter events, 26.8 us)
Async XLA Ops:
  0.6 1.1 copy-start
  3.1 7.4 %copy-start.7 = (bf16[8,16,2048]{2,1,0:T(8,128)(2,1)S(1)}, bf16[8,16,2048]{2,1,0:T(8,128)(2,1)}, u32[]{:S(2)}) copy-start(bf16[8,16,2048]{2,1,0:T(8,128)(2,1)} %param.9) | copy-start | bytes 1572868
  3.1 21.9 %all-to-all-start.3 = ((bf16[8,16,2048]{2,1,0:T(8,128)(2,1)}), bf16[8,16,2048]{2,1,0:T(8,128)(2,1)S(1)}, u32[]{:S(2)}, u32[]{:S(2)}) async-start(bf16[8,16,2048]{2,1,0:T(8,128)(2,1)} %gather_fusion.3), calls=%async_computation.3 | async-start | bytes 1048576 | tf_op jit(solution)/shard_map/all_to_all | solution.py:123
  24.9 7.6 %copy-start.8 = (bf16[8,16,256]{2,1,0:T(8,128)(2,1)S(1)}, bf16[8,16,256]{2,1,0:T(8,128)(2,1)}, u32[]{:S(2)}) copy-start(bf16[8,16,256]{2,1,0:T(8,128)(2,1)} %param.11) | copy-start | bytes 196612
  24.9 75.9 %all-to-all-start = ((bf16[8,16,2048]{2,1,0:T(8,128)(2,1)}), bf16[8,16,2048]{2,1,0:T(8,128)(2,1)S(1)}, u32[]{:S(2)}, u32[]{:S(2)}) async-start(bf16[8,16,2048]{2,1,0:T(8,128)(2,1)} %gather_fusion), calls=%async_computation | async-start | bytes 1048576 | tf_op jit(solution)/shard_map/all_to_all | solution.py:120
  30.6 0.7 copy-start.13
  32.5 1.2 copy-start.9
  33.7 1.2 copy-start.10
  66.1 0.7 copy-start.11
  100.8 12.1 %all-to-all-start.1 = ((bf16[8,16,256]{2,1,0:T(8,128)(2,1)}), bf16[8,16,256]{2,1,0:T(8,128)(2,1)S(1)}, u32[]{:S(2)}, u32[]{:S(2)}) async-start(bf16[8,16,256]{2,1,0:T(8,128)(2,1)} %gather_fusion.1), calls=%async_computation.1 | async-start | bytes 131072 | tf_op jit(solution)/shard_map/all_to_all | solution.py:121
  112.9 10.4 %all-to-all-start.2 = ((bf16[8,16,256]{2,1,0:T(8,128)(2,1)}), bf16[8,16,256]{2,1,0:T(8,128)(2,1)S(1)}, u32[]{:S(2)}, u32[]{:S(2)}) async-start(bf16[8,16,256]{2,1,0:T(8,128)(2,1)} %gather_fusion.2), calls=%async_computation.2 | async-start | bytes 131072 | tf_op jit(solution)/shard_map/all_to_all | solution.py:122
  117.0 9.0 %copy-start.1 = (f32[224,128]{1,0:T(8,128)}, f32[224,128]{1,0:T(8,128)S(1)}, u32[]{:S(2)}) copy-start(f32[224,128]{1,0:T(8,128)S(1)} %convolution_bitcast_fusion) | copy-start | bytes 344068
  124.4 10.1 %copy-start.5 = (f32[224,128]{1,0:T(8,128)}, f32[224,128]{1,0:T(8,128)S(1)}, u32[]{:S(2)}) copy-start(f32[224,128]{1,0:T(8,128)S(1)} %fusion.12) | copy-start | bytes 344068
  129.0 10.9 %all-to-all-start.6 = ((bf16[8,2,2048]{2,1,0:T(2,128)(2,1)}), bf16[8,2,2048]{2,1,0:T(2,128)(2,1)}, u32[]{:S(2)}, u32[]{:S(2)}) async-start(bf16[8,2,2048]{2,1,0:T(2,128)(2,1)} %reshape.232), calls=%async_computation.6 | async-start | bytes 131072 | tf_op jit(solution)/shard_map/all_to_all | solution.py:175
  139.9 10.2 %all-to-all-start.5 = ((bf16[8,2,2048]{2,1,0:T(2,128)(2,1)}), bf16[8,2,2048]{2,1,0:T(2,128)(2,1)S(1)}, u32[]{:S(2)}, u32[]{:S(2)}) async-start(bf16[8,2,2048]{2,1,0:T(2,128)(2,1)} %reshape.230), calls=%async_computation.5 | async-start | bytes 131072 | tf_op jit(solution)/shard_map/all_to_all | solution.py:168
  149.2 6.1 %copy-start.15 = (s32[8]{0:T(128)S(1)}, s32[8]{0:T(128)}, u32[]{:S(2)}) copy-start(s32[8]{0:T(128)} %param.16) | copy-start | bytes 100
  149.2 6.1 %copy-start.2 = (f32[224,128]{1,0:T(8,128)S(1)}, f32[224,128]{1,0:T(8,128)}, u32[]{:S(2)}) copy-start(f32[224,128]{1,0:T(8,128)} %copy-done.1) | copy-start | bytes 344068
  149.2 6.1 %copy-start.4 = (f32[224,128]{1,0:T(8,128)S(1)}, f32[224,128]{1,0:T(8,128)}, u32[]{:S(2)}) copy-start(f32[224,128]{1,0:T(8,128)} %copy-done.3) | copy-start | bytes 344068
  149.2 6.1 %copy-start.6 = (f32[224,128]{1,0:T(8,128)S(1)}, f32[224,128]{1,0:T(8,128)}, u32[]{:S(2)}) copy-start(f32[224,128]{1,0:T(8,128)} %copy-done.5) | copy-start | bytes 344068
  150.1 44.4 %all-to-all-start.4 = ((bf16[8,2,16384]{2,1,0:T(2,128)(2,1)}), bf16[8,2,16384]{2,1,0:T(2,128)(2,1)S(1)}, u32[]{:S(2)}, u32[]{:S(2)}) async-start(bf16[8,2,16384]{2,1,0:T(2,128)(2,1)} %reshape.228), calls=%async_computation.4 | async-start | bytes 1048576 | tf_op jit(solution)/shard_map/all_to_all | solution.py:165
  178.9 10.4 %collective-permute-start.2 = (bf16[16,256]{1,0:T(8,128)(2,1)S(1)}, bf16[16,256]{1,0:T(8,128)(2,1)S(1)}, u32[]{:S(2)}, u32[]{:S(2)}) collective-permute-start(bf16[16,256]{1,0:T(8,128)(2,1)S(1)} %convert.44), channel_id=1, source_target_pairs={{0,2},{2,4},{4,6},{6,8},{8,10},{10,12},{12,14},{1,3},{3,5},{5,7},{... | collective-permute-start | bytes 24584
  180.9 8.4 %collective-permute-start.3 = (bf16[12,256]{1,0:T(8,128)(2,1)S(1)}, bf16[12,256]{1,0:T(8,128)(2,1)S(1)}, u32[]{:S(2)}, u32[]{:S(2)}) collective-permute-start(bf16[12,256]{1,0:T(8,128)(2,1)S(1)} %slice.83), channel_id=1, source_target_pairs={{0,4},{2,6},{4,8},{6,10},{8,12},{10,14},{1,5},{3,7},{5,9},{7,11},{... | collective-permute-start | bytes 18440
  182.2 7.4 %collective-permute-start = (bf16[16,256]{1,0:T(8,128)(2,1)S(1)}, bf16[16,256]{1,0:T(8,128)(2,1)S(1)}, u32[]{:S(2)}, u32[]{:S(2)}) collective-permute-start(bf16[16,256]{1,0:T(8,128)(2,1)S(1)} %convert.43), channel_id=1, source_target_pairs={{0,2},{2,4},{4,6},{6,8},{8,10},{10,12},{12,14},{1,3},{3,5},{5,7},{... | collective-permute-start | bytes 24584
  185.4 4.2 %collective-permute-start.1 = (bf16[12,256]{1,0:T(8,128)(2,1)S(1)}, bf16[12,256]{1,0:T(8,128)(2,1)S(1)}, u32[]{:S(2)}, u32[]{:S(2)}) collective-permute-start(bf16[12,256]{1,0:T(8,128)(2,1)S(1)} %slice.82), channel_id=1, source_target_pairs={{0,4},{2,6},{4,8},{6,10},{8,12},{10,14},{1,5},{3,7},{5,9},{7,11},{... | collective-permute-start | bytes 18440
  (3 other events, 2.0 us)
where the time goes:
time: 198 us; the launch traced here: 197 us
  blocking collectives  85.2 us (43%)
  starting transfers between devices  41.6 us (21%)
  waiting for transfers between devices  30 us (15%)
  local copies, waits for them, and re-layouts  22.9 us (12%)
  other arithmetic  9.71 us (5%)
  between operations  3.84 us (2%)
  matrix products  3.45 us (2%)
    all_gather x1, blocking collectives, body(): lax.all_gather(prompt_key, 'seq', axis=0, tiled=True)  31.2 us
    all_gather x1, blocking collectives, body(): lax.all_gather(prompt_value, 'seq', axis=0, tiled=True)  30.5 us
    unnamed x1, blocking collectives  23.4 us
    all_to_all x1, waiting for transfers between devices, body(): lax.all_to_all(response_grad[resident], 'seq', split_axis=0, concat_axis=...  13.1 us
    unnamed x4, starting transfers between devices  9.32 us
    unnamed x50, local copies, waits for them, and re-layouts  9.2 us
    all_to_all x1, starting transfers between devices, body(): lax.all_to_all(response_grad[resident], 'seq', split_axis=0, concat_axis=...  7.38 us
    unnamed x6, other arithmetic  6.82 us
  transfers between devices with their start and end apart: 11, of which 5 were waited for; matrix products, arithmetic and copies ran while one was open for 24% of the time, Pallas kernels for 0%

commit v1 on v0

--- a/solution.py
+++ b/solution.py
@@ -1,6 +1,10 @@
+import functools
+
 import jax
 import jax.numpy as jnp
 from jax import lax
+from jax.experimental import pallas as pl
+from jax.experimental.pallas import tpu as pltpu
 from jax.sharding import PartitionSpec as P
 
 HEAD_DIM = 128
@@ -98,7 +102,7 @@
     )
 
 
-def body(
+def collective_body(
     response_query,
     response_key,
     response_value,
@@ -190,6 +194,258 @@
     )
 
 
+ROW_TILE = 16
+MESH = pl.DeviceIdType.MESH
+
+
+def dot_last(left, right):
+    return lax.dot_general(left, right, (((1,), (1,)), ((), ())), preferred_element_type=jnp.float32)
+
+
+def dot_first(left, right):
+    return lax.dot_general(left, right, (((0,), (0,)), ((), ())), preferred_element_type=jnp.float32)
+
+
+def dot_plain(left, right):
+    return lax.dot_general(left, right, (((1,), (0,)), ((), ())), preferred_element_type=jnp.float32)
+
+
+def wait_bytes(ref, sem):
+    pltpu.make_async_copy(ref, ref, sem).wait()
+
+
+def kernel(
+    n, pieces, prompt_rows,
+    q_ref, k_ref, v_ref, g_ref, pk_ref, pv_ref, len_ref, home_ref, seen_ref,
+    out_ref, dq_ref, dk_ref, dv_ref, dpk_ref, dpv_ref,
+    send_qg, send_kv, in_qg, in_kv, grad_q, grad_kv, back_q, back_kv, acc,
+    sem_send, sem_kv, sem_qg, sem_back,
+):
+    me = lax.axis_index("seq")
+    rows = q_ref.shape[1]
+    width = q_ref.shape[2]
+    kv_width = k_ref.shape[2]
+    kv_heads = kv_width // HEAD_DIM
+    heads = width // HEAD_DIM
+    group = heads // kv_heads
+    total = n * rows
+    slot = in_kv.shape[1] // n
+    scale = 1.0 / HEAD_DIM**0.5
+
+    barrier = pltpu.get_barrier_semaphore()
+    for step in range(1, n):
+        pl.semaphore_signal(
+            barrier, inc=1, device_id={"seq": lax.rem(me + step, n)}, device_id_type=MESH
+        )
+
+    def resident(rank):
+        found = jnp.int32(0)
+        for r in range(n):
+            found = jnp.where(home_ref[r] == rank, jnp.int32(r), found)
+        return found
+
+    def pair_cols(head):
+        return head * 2 * HEAD_DIM, head * 2 * HEAD_DIM + HEAD_DIM
+
+    prompt_pad = jnp.zeros((slot - prompt_rows, HEAD_DIM), jnp.float32)
+    for rank in range(n):
+        source = resident(rank)
+        send_qg[rank, 0] = q_ref[source]
+        send_qg[rank, 1] = g_ref[source]
+        key_rows = k_ref[source]
+        value_rows = v_ref[source]
+        for h in range(kv_heads):
+            kc, vc = pair_cols(h)
+            own = slice(h * HEAD_DIM, (h + 1) * HEAD_DIM)
+            send_kv[rank, 0, :, kc : kc + HEAD_DIM] = key_rows[:, own]
+            send_kv[rank, 0, :, vc : vc + HEAD_DIM] = value_rows[:, own]
+            for ref, col in ((pk_ref, kc), (pv_ref, vc)):
+                part = ref[:, own].astype(jnp.float32)
+                if slot > prompt_rows:
+                    part = jnp.concatenate([part, prompt_pad], axis=0)
+                send_kv[rank, 1, :, col : col + HEAD_DIM] = part.astype(jnp.bfloat16)
+
+    pl.semaphore_wait(barrier, n - 1)
+
+    own_rows = pl.ds(pl.multiple_of(me * rows, rows), rows)
+    own_slots = pl.ds(pl.multiple_of(me * slot, slot), slot)
+    piece_width = width // pieces
+    for step in range(1, n):
+        peer = lax.rem(me + step, n)
+        pltpu.make_async_remote_copy(
+            src_ref=send_kv.at[peer], dst_ref=in_kv.at[:, own_slots, :],
+            send_sem=sem_send.at[0], recv_sem=sem_kv,
+            device_id={"seq": peer}, device_id_type=MESH,
+        ).start()
+    for piece in range(pieces):
+        cols = pl.ds(piece * piece_width, piece_width)
+        for step in range(1, n):
+            peer = lax.rem(me + step, n)
+            pltpu.make_async_remote_copy(
+                src_ref=send_qg.at[peer, :, :, cols], dst_ref=in_qg.at[:, own_rows, cols],
+                send_sem=sem_send.at[1], recv_sem=sem_qg.at[piece],
+                device_id={"seq": peer}, device_id_type=MESH,
+            ).start()
+    in_kv[:, own_slots, :] = send_kv[me]
+    in_qg[:, own_rows, :] = send_qg[me]
+
+    own = resident(me)
+    length = len_ref[own]
+    visible = seen_ref[own]
+    keys_total = total + n * slot
+    row_id = lax.broadcasted_iota(jnp.int32, (total, keys_total), 0)
+    col_id = lax.broadcasted_iota(jnp.int32, (total, keys_total), 1)
+    in_prompt = col_id - total
+    prompt_slot = in_prompt // slot
+    prompt_row = in_prompt - prompt_slot * slot
+    prompt_id = prompt_slot * prompt_rows + prompt_row
+    allowed = jnp.where(
+        col_id < total,
+        (col_id <= row_id).astype(jnp.int32),
+        ((prompt_row < prompt_rows) & (prompt_id < visible)).astype(jnp.int32),
+    ) > 0
+    live = lax.broadcasted_iota(jnp.int32, (total, HEAD_DIM), 0) < length
+
+    wait_bytes(in_kv.at[:, 0 : (n - 1) * slot, :], sem_kv)
+    per_piece = heads // pieces
+    pieces_per_kv = group // per_piece
+    for piece in range(pieces):
+        cols = pl.ds(piece * piece_width, piece_width)
+        h = piece // pieces_per_kv
+        kc, vc = pair_cols(h)
+        keys = in_kv[:, :, kc : kc + HEAD_DIM].reshape(keys_total, HEAD_DIM)
+        values = in_kv[:, :, vc : vc + HEAD_DIM].reshape(keys_total, HEAD_DIM)
+        wait_bytes(in_qg.at[:, 0 : (n - 1) * rows, cols], sem_qg.at[piece])
+        for a in range(per_piece):
+            low = piece * piece_width + a * HEAD_DIM
+            head_cols = slice(low, low + HEAD_DIM)
+            query = in_qg[0, :, head_cols]
+            grad_wide = jnp.where(live, in_qg[1, :, head_cols].astype(jnp.float32), 0.0)
+            grad = grad_wide.astype(jnp.bfloat16)
+            logits = jnp.where(allowed, dot_last(query, keys) * scale, NEG_FILL)
+            exped = jnp.exp(logits - jnp.max(logits, axis=1, keepdims=True))
+            prob = exped * (1.0 / jnp.sum(exped, axis=1, keepdims=True))
+            weights = prob.astype(jnp.bfloat16)
+            output = jnp.where(live, dot_plain(weights, values), 0.0).astype(jnp.bfloat16)
+            out_ref[0, :, head_cols] = output
+            row_dot = jnp.sum(grad_wide * output.astype(jnp.float32), axis=1, keepdims=True)
+            dlogit = (prob * (dot_last(grad, values) - row_dot)).astype(jnp.bfloat16)
+            grad_q[:, head_cols] = (dot_plain(dlogit, keys) * scale).astype(jnp.bfloat16)
+            dkey = dot_first(dlogit, query)
+            dvalue = dot_first(weights, grad)
+            if piece % pieces_per_kv == 0 and a == 0:
+                acc[0] = dkey
+                acc[1] = dvalue
+            else:
+                acc[0] += dkey
+                acc[1] += dvalue
+        for step in range(1, n):
+            peer = lax.rem(me + step, n)
+            pltpu.make_async_remote_copy(
+                src_ref=grad_q.at[pl.ds(pl.multiple_of(peer * rows, rows), rows), cols],
+                dst_ref=back_q.at[me, :, cols],
+                send_sem=sem_send.at[2], recv_sem=sem_back.at[0],
+                device_id={"seq": peer}, device_id_type=MESH,
+            ).start()
+        if piece % pieces_per_kv == pieces_per_kv - 1:
+            dkey = (acc[0] * scale).astype(jnp.bfloat16)
+            dvalue = acc[1].astype(jnp.bfloat16)
+            for col, part in ((kc, dkey), (vc, dvalue)):
+                grad_kv[0, :, col : col + HEAD_DIM] = part[:total]
+                grad_kv[1, :, col : col + HEAD_DIM] = part[total:]
+            pair = pl.ds(kc, 2 * HEAD_DIM)
+            for step in range(1, n):
+                peer = lax.rem(me + step, n)
+                pltpu.make_async_remote_copy(
+                    src_ref=grad_kv.at[:, pl.ds(pl.multiple_of(peer * slot, slot), slot), pair],
+                    dst_ref=back_kv.at[me, :, :, pair],
+                    send_sem=sem_send.at[3], recv_sem=sem_back.at[1],
+                    device_id={"seq": peer}, device_id_type=MESH,
+                ).start()
+    back_q[me] = grad_q[own_rows, :]
+    back_kv[me] = grad_kv[:, own_slots, :]
+
+    wait_bytes(back_q.at[0 : n - 1], sem_back.at[0])
+    for r in range(n):
+        dq_ref[r] = back_q[home_ref[r]]
+    wait_bytes(back_kv.at[0 : n - 1], sem_back.at[1])
+    for r in range(n):
+        home = home_ref[r]
+        pair_grad = back_kv[home, 0]
+        for h in range(kv_heads):
+            kc, vc = pair_cols(h)
+            own = slice(h * HEAD_DIM, (h + 1) * HEAD_DIM)
+            dk_ref[r, :, own] = pair_grad[:, kc : kc + HEAD_DIM]
+            dv_ref[r, :, own] = pair_grad[:, vc : vc + HEAD_DIM]
+    prompt_sum = back_kv[0, 1].astype(jnp.float32)
+    for rank in range(1, n):
+        prompt_sum = prompt_sum + back_kv[rank, 1].astype(jnp.float32)
+    for h in range(kv_heads):
+        kc, vc = pair_cols(h)
+        own = slice(h * HEAD_DIM, (h + 1) * HEAD_DIM)
+        dpk_ref[:, own] = prompt_sum[:prompt_rows, kc : kc + HEAD_DIM].astype(jnp.bfloat16)
+        dpv_ref[:, own] = prompt_sum[:prompt_rows, vc : vc + HEAD_DIM].astype(jnp.bfloat16)
+
+    wait_bytes(send_kv.at[0 : n - 1], sem_send.at[0])
+    wait_bytes(send_qg.at[0 : n - 1], sem_send.at[1])
+    wait_bytes(back_q.at[0 : n - 1], sem_send.at[2])
+    wait_bytes(back_kv.at[0 : n - 1], sem_send.at[3])
+
+
+def kernel_body(*arrays):
+    query, key, _, _, prompt_key, _, _, _, _ = arrays
+    n = lax.axis_size("seq")
+    rows, width = query.shape[1:]
+    kv_width = key.shape[2]
+    prompt_rows = prompt_key.shape[0]
+    slot = -(-prompt_rows // ROW_TILE) * ROW_TILE
+    group = width // kv_width
+    pieces = (kv_width // HEAD_DIM) * (2 if group % 2 == 0 else 1)
+    total = n * rows
+    bf16 = jnp.bfloat16
+    vmem = pl.BlockSpec(memory_space=pltpu.VMEM)
+    smem = pl.BlockSpec(memory_space=pltpu.SMEM)
+    return pl.pallas_call(
+        functools.partial(kernel, n, pieces, prompt_rows),
+        out_shape=(
+            jax.ShapeDtypeStruct((1, total, width), bf16),
+            jax.ShapeDtypeStruct(query.shape, bf16),
+            jax.ShapeDtypeStruct(key.shape, bf16),
+            jax.ShapeDtypeStruct(key.shape, bf16),
+            jax.ShapeDtypeStruct(prompt_key.shape, bf16),
+            jax.ShapeDtypeStruct(prompt_key.shape, bf16),
+        ),
+        in_specs=[vmem] * 6 + [smem] * 3,
+        out_specs=(vmem,) * 6,
+        scratch_shapes=[
+            pltpu.VMEM((n, 2, rows, width), bf16),
+            pltpu.VMEM((n, 2, rows, 2 * kv_width), bf16),
+            pltpu.VMEM((2, total, width), bf16),
+            pltpu.VMEM((2, total, 2 * kv_width), bf16),
+            pltpu.VMEM((total, width), bf16),
+            pltpu.VMEM((2, total, 2 * kv_width), bf16),
+            pltpu.VMEM((n, rows, width), bf16),
+            pltpu.VMEM((n, 2, rows, 2 * kv_width), bf16),
+            pltpu.VMEM((2, total + n * slot, HEAD_DIM), jnp.float32),
+            pltpu.SemaphoreType.DMA((4,)),
+            pltpu.SemaphoreType.DMA,
+            pltpu.SemaphoreType.DMA((pieces,)),
+            pltpu.SemaphoreType.DMA((2,)),
+        ],
+        compiler_params=pltpu.CompilerParams(
+            collective_id=0, has_side_effects=True, vmem_limit_bytes=40 * 1024 * 1024
+        ),
+    )(*arrays)
+
+
+def body(*arrays):
+    rows = arrays[0].shape[1]
+    slot = -(-arrays[4].shape[0] // ROW_TILE) * ROW_TILE
+    if rows % ROW_TILE == 0 and slot == rows:
+        return kernel_body(*arrays)
+    return collective_body(*arrays)
+
+
 def solution(mesh):
     placed = (
         P("group", "seq", "head"),

time: 198 us -> 65.4 us (0.33)
  blocking collectives: 85.2 us -> 0 us
  Pallas kernels: 0 us -> 53.1 us
  starting transfers between devices: 41.6 us -> 0 us
  waiting for transfers between devices: 30 us -> 0 us
  local copies, waits for them, and re-layouts: 22.9 us -> 11.2 us
  other arithmetic: 9.71 us -> 0 us
  matrix products: 3.45 us -> 0 us
  between operations: 3.84 us -> 0.66 us
    all_gather x2 -> x0, blocking collectives: 61.8 us -> none  [the longest x1 31.2 us: body(): lax.all_gather(prompt_key, 'seq', axis=0, tiled=True)]
    pallas_call x0 -> x1, Pallas kernels: none -> 53.1 us  [kernel_body(): pl.pallas_call(functools.partial(kernel, n, pieces, prompt_rows), out_sha...]
    all_to_all x7 -> x0, starting transfers between devices: 32.3 us -> none  [the longest x1 7.38 us: body(): lax.all_to_all(response_grad[resident], 'seq', split_axis=0, concat_axis=...]
    all_to_all x7 -> x0, waiting for transfers between devices: 30 us -> none  [the longest x1 13.1 us: body(): lax.all_to_all(response_grad[resident], 'seq', split_axis=0, concat_axis=...]
    unnamed x1 -> x0, blocking collectives: 23.4 us -> none
    unnamed x4 -> x0, starting transfers between devices: 9.32 us -> none
    gather x7 -> x0, local copies, waits for them, and re-layouts: 8.83 us -> none  [the longest x1 1.37 us: body(): response_query[resident]]
    unnamed x6 -> x0, other arithmetic: 6.82 us -> none
  transfers between devices with their start and end apart: 11 -> 0, of which waited for: 5 -> 0; matrix products, arithmetic and copies ran while one was open for 24% -> 0% of each run, Pallas kernels for 0% -> 0%
where the time goes in v1:
time: 65.4 us; the launch traced here: 65 us
  Pallas kernels  53.1 us (81%)
  local copies, waits for them, and re-layouts  11.2 us (17%)
  between operations  0.66 us (1%)
    pallas_call x1, Pallas kernels, kernel_body(): pl.pallas_call(functools.partial(kernel, n, pieces, prompt_rows), out_sha...  53.1 us
    unnamed x24, local copies, waits for them, and re-layouts  11.2 us

profile of v1, /device:TPU:0, one launch (start us, length us, event | category | flops | bytes accessed | tf_op | source)
XLA Modules:
  0.0 65.0 jit_solution(11383077659674507413)
XLA Ops:
  0.6 0.0 copy-start
  0.6 1.0 %copy-done = bf16[8,16,2048]{2,1,0:T(8,128)(2,1)S(1)} copy-done((bf16[8,16,2048]{2,1,0:T(8,128)(2,1)S(1)}, bf16[8,16,2048]{2,1,0:T(8,128)(2,1)}, u32[]{:S(2)}) %copy-start) | copy-done | bytes 524312
  1.7 0.0 copy-start.1
  1.7 1.0 %copy-done.1 = bf16[8,16,2048]{2,1,0:T(8,128)(2,1)S(1)} copy-done((bf16[8,16,2048]{2,1,0:T(8,128)(2,1)S(1)}, bf16[8,16,2048]{2,1,0:T(8,128)(2,1)}, u32[]{:S(2)}) %copy-start.1) | copy-done | bytes 524312
  2.7 0.0 copy-start.2
  2.7 0.8 %copy-done.2 = bf16[8,16,256]{2,1,0:T(8,128)(2,1)S(1)} copy-done((bf16[8,16,256]{2,1,0:T(8,128)(2,1)S(1)}, bf16[8,16,256]{2,1,0:T(8,128)(2,1)}, u32[]{:S(2)}) %copy-start.2) | copy-done | bytes 65560
  3.6 0.0 copy-start.3
  3.6 0.8 %copy-done.3 = bf16[8,16,256]{2,1,0:T(8,128)(2,1)S(1)} copy-done((bf16[8,16,256]{2,1,0:T(8,128)(2,1)S(1)}, bf16[8,16,256]{2,1,0:T(8,128)(2,1)}, u32[]{:S(2)}) %copy-start.3) | copy-done | bytes 65560
  4.4 0.0 copy-start.4
  4.4 0.7 %copy-done.4 = bf16[12,256]{1,0:T(8,128)(2,1)S(1)} copy-done((bf16[12,256]{1,0:T(8,128)(2,1)S(1)}, bf16[12,256]{1,0:T(8,128)(2,1)}, u32[]{:S(2)}) %copy-start.4) | copy-done | bytes 6168
  5.1 0.0 copy-start.5
  5.1 0.7 %copy-done.5 = bf16[12,256]{1,0:T(8,128)(2,1)S(1)} copy-done((bf16[12,256]{1,0:T(8,128)(2,1)S(1)}, bf16[12,256]{1,0:T(8,128)(2,1)}, u32[]{:S(2)}) %copy-start.5) | copy-done | bytes 6168
  5.8 0.0 copy-start.6
  5.8 0.7 %copy-done.6 = s32[8]{0:T(128)S(1)} copy-done((s32[8]{0:T(128)S(1)}, s32[8]{0:T(128)}, u32[]{:S(2)}) %copy-start.6) | copy-done | bytes 56
  6.5 0.0 copy-start.7
  6.5 0.7 %copy-done.7 = s32[8]{0:T(128)S(1)} copy-done((s32[8]{0:T(128)S(1)}, s32[8]{0:T(128)}, u32[]{:S(2)}) %copy-start.7) | copy-done | bytes 56
  7.1 0.7 %copy-done.8 = s32[8]{0:T(128)S(1)} copy-done((s32[8]{0:T(128)S(1)}, s32[8]{0:T(128)}, u32[]{:S(2)}) %copy-start.8) | copy-done | bytes 56
  7.8 53.1 %shard_map.136 = (bf16[1,128,2048]{2,1,0:T(8,128)(2,1)S(1)}, bf16[8,16,2048]{2,1,0:T(8,128)(2,1)S(1)}, bf16[8,16,256]{2,1,0:T(8,128)(2,1)S(1)}, bf16[8,16,256]{2...) custom-call(bf16[8,16,2048]{2,1,0:T(8,128)(2,1)S(1)} %copy-done, ...), custom_call_target="tpu_custom_call" | custom-call | tf_op jit(solution)/shard_map/pallas_call | solution.py:408
  60.9 0.8 %copy.21 = bf16[1,128,2048]{2,1,0:T(8,128)(2,1)} copy(bf16[1,128,2048]{2,1,0:T(8,128)(2,1)S(1)} %get-tuple-element.12) | data formatting | bytes 1048576
  61.7 0.8 %copy.22 = bf16[8,16,2048]{2,1,0:T(8,128)(2,1)} copy(bf16[8,16,2048]{2,1,0:T(8,128)(2,1)S(1)} %get-tuple-element.13) | data formatting | bytes 1048576
  62.5 0.6 copy.23
  63.1 0.6 copy.24
  63.8 0.6 copy.25
  64.4 0.6 copy.26
  (1 shorter events, 0.0 us)
Async XLA Ops:
  0.6 1.0 %copy-start = (bf16[8,16,2048]{2,1,0:T(8,128)(2,1)S(1)}, bf16[8,16,2048]{2,1,0:T(8,128)(2,1)}, u32[]{:S(2)}) copy-start(bf16[8,16,2048]{2,1,0:T(8,128)(2,1)} %q_ref.1) | copy-start | bytes 1572868
  1.7 1.0 %copy-start.1 = (bf16[8,16,2048]{2,1,0:T(8,128)(2,1)S(1)}, bf16[8,16,2048]{2,1,0:T(8,128)(2,1)}, u32[]{:S(2)}) copy-start(bf16[8,16,2048]{2,1,0:T(8,128)(2,1)} %g_ref.1) | copy-start | bytes 1572868
  2.7 0.8 %copy-start.2 = (bf16[8,16,256]{2,1,0:T(8,128)(2,1)S(1)}, bf16[8,16,256]{2,1,0:T(8,128)(2,1)}, u32[]{:S(2)}) copy-start(bf16[8,16,256]{2,1,0:T(8,128)(2,1)} %k_ref.1) | copy-start | bytes 196612
  3.6 0.8 %copy-start.3 = (bf16[8,16,256]{2,1,0:T(8,128)(2,1)S(1)}, bf16[8,16,256]{2,1,0:T(8,128)(2,1)}, u32[]{:S(2)}) copy-start(bf16[8,16,256]{2,1,0:T(8,128)(2,1)} %v_ref.1) | copy-start | bytes 196612
  4.4 0.7 %copy-start.4 = (bf16[12,256]{1,0:T(8,128)(2,1)S(1)}, bf16[12,256]{1,0:T(8,128)(2,1)}, u32[]{:S(2)}) copy-start(bf16[12,256]{1,0:T(8,128)(2,1)} %pk_ref.1) | copy-start | bytes 18436
  5.1 0.7 %copy-start.5 = (bf16[12,256]{1,0:T(8,128)(2,1)S(1)}, bf16[12,256]{1,0:T(8,128)(2,1)}, u32[]{:S(2)}) copy-start(bf16[12,256]{1,0:T(8,128)(2,1)} %pv_ref.1) | copy-start | bytes 18436
  5.8 0.7 %copy-start.6 = (s32[8]{0:T(128)S(1)}, s32[8]{0:T(128)}, u32[]{:S(2)}) copy-start(s32[8]{0:T(128)} %len_ref.1) | copy-start | bytes 100
  6.5 0.7 %copy-start.7 = (s32[8]{0:T(128)S(1)}, s32[8]{0:T(128)}, u32[]{:S(2)}) copy-start(s32[8]{0:T(128)} %home_ref.1) | copy-start | bytes 100
  7.1 0.7 %copy-start.8 = (s32[8]{0:T(128)S(1)}, s32[8]{0:T(128)}, u32[]{:S(2)}) copy-start(s32[8]{0:T(128)} %seen_ref.1) | copy-start | bytes 100

commit v2 on v0

--- a/solution.py
+++ b/solution.py
@@ -1,6 +1,10 @@
+import functools
+
 import jax
 import jax.numpy as jnp
 from jax import lax
+from jax.experimental import pallas as pl
+from jax.experimental.pallas import tpu as pltpu
 from jax.sharding import PartitionSpec as P
 
 HEAD_DIM = 128
@@ -98,7 +102,7 @@
     )
 
 
-def body(
+def collective_body(
     response_query,
     response_key,
     response_value,
@@ -190,6 +194,387 @@
     )
 
 
+ROW_TILE = 16
+MESH = pl.DeviceIdType.MESH
+
+
+def dot_last(left, right):
+    return lax.dot_general(left, right, (((1,), (1,)), ((), ())), preferred_element_type=jnp.float32)
+
+
+def dot_first(left, right):
+    return lax.dot_general(left, right, (((0,), (0,)), ((), ())), preferred_element_type=jnp.float32)
+
+
+def dot_plain(left, right):
+    return lax.dot_general(left, right, (((1,), (0,)), ((), ())), preferred_element_type=jnp.float32)
+
+
+def wait_bytes(ref, sem):
+    pltpu.make_async_copy(ref, ref, sem).wait()
+
+
+def kernel(
+    n, inner, prompt_rows,
+    q_hbm, k_hbm, v_hbm, g_hbm, pk_ref, pv_ref, len_hbm, home_hbm, seen_hbm,
+    out_ref, back_q, dk_ref, dv_ref, dpk_ref, dpv_ref,
+    q_ref, k_ref, v_ref, g_ref, len_ref, home_ref, seen_ref,
+    send_qg, send_kv, send_p, in_qg, in_kv, in_p,
+    out_send, grad_q, grad_kv, grad_p, back_kv, back_p, acc,
+    sem_load, sem_local, sem_send, sem_kv_out, sem_grad_out,
+    sem_p, sem_qg, sem_kv, sem_out, sem_q, sem_grad, sem_gp,
+):
+    me = lax.axis_index("seq")
+    outer = n // inner
+    mz, mx = lax.div(me, inner), lax.rem(me, inner)
+    rows, width = q_ref.shape[1:]
+    kv_width = k_ref.shape[2]
+    kv_heads = kv_width // HEAD_DIM
+    group = width // kv_width
+    total = n * rows
+    block = inner * rows
+    stacked = group * block
+    slot = in_p.shape[0] // n
+    scale = 1.0 / HEAD_DIM**0.5
+
+    loads = [
+        pltpu.make_async_copy(src, dst, sem_load.at[i])
+        for i, (src, dst) in enumerate((
+            (len_hbm, len_ref), (home_hbm, home_ref), (seen_hbm, seen_ref),
+            (k_hbm, k_ref), (v_hbm, v_ref), (q_hbm, q_ref), (g_hbm, g_ref),
+        ))
+    ]
+    for load in loads:
+        load.start()
+    in_kv[...] = jnp.zeros_like(in_kv)
+    back_kv[...] = jnp.zeros_like(back_kv)
+    barrier = pltpu.get_barrier_semaphore()
+    for step in range(1, n):
+        pl.semaphore_signal(
+            barrier, inc=1, device_id={"seq": lax.rem(me + step, n)}, device_id_type=MESH
+        )
+
+    def send(src, dst, send_sem, recv_sem, peer):
+        pltpu.make_async_remote_copy(
+            src_ref=src, dst_ref=dst, send_sem=send_sem, recv_sem=recv_sem,
+            device_id={"seq": peer}, device_id_type=MESH,
+        ).start()
+
+    def tile(index, size):
+        return pl.ds(pl.multiple_of(index * size, size), size)
+
+    def pair_cols(head):
+        return head * 2 * HEAD_DIM, head * 2 * HEAD_DIM + HEAD_DIM
+
+    prompt_pad = jnp.zeros((slot - prompt_rows, HEAD_DIM), jnp.float32)
+    for h in range(kv_heads):
+        kc, vc = pair_cols(h)
+        own = slice(h * HEAD_DIM, (h + 1) * HEAD_DIM)
+        for ref, col in ((pk_ref, kc), (pv_ref, vc)):
+            part = ref[:, own].astype(jnp.float32)
+            if slot > prompt_rows:
+                part = jnp.concatenate([part, prompt_pad], axis=0)
+            send_p[:, col : col + HEAD_DIM] = part.astype(jnp.bfloat16)
+    for load in loads[:5]:
+        load.wait()
+
+    def resident(rank):
+        found = jnp.int32(0)
+        for r in range(n):
+            found = jnp.where(home_ref[r] == rank, jnp.int32(r), found)
+        return found
+
+    sources = [resident(rank) for rank in range(n)]
+    for rank in range(n):
+        key_rows = k_ref[sources[rank]]
+        value_rows = v_ref[sources[rank]]
+        for h in range(kv_heads):
+            kc, vc = pair_cols(h)
+            own = slice(h * HEAD_DIM, (h + 1) * HEAD_DIM)
+            send_kv[rank, :, kc : kc + HEAD_DIM] = key_rows[:, own]
+            send_kv[rank, :, vc : vc + HEAD_DIM] = value_rows[:, own]
+    pl.semaphore_wait(barrier, n - 1)
+
+    partner = mz * inner + (inner - 1 - mx)
+    own_rows = tile(me, rows)
+
+    def send_keys(stage):
+        for step in range(outer):
+            @pl.when(mz + step < outer)
+            def _():
+                for dx in range(inner):
+                    home = stage * inner + dx
+                    peer = (mz + step) * inner + dx
+
+                    def go():
+                        send(send_kv.at[home], in_kv.at[stage, own_rows, :],
+                             sem_kv_out.at[step], sem_kv.at[stage, mz], peer)
+
+                    if step == 0:
+                        pl.when(mx != dx)(go)
+                    else:
+                        go()
+
+    send_keys(0)
+    for step in range(1, n):
+        send(send_p, in_p.at[tile(me, slot), :], sem_send.at[0], sem_p, lax.rem(me + step, n))
+    loads[5].wait()
+    loads[6].wait()
+    for stage in range(outer):
+        for dx in range(inner):
+            rank = stage * inner + dx
+            send_qg[rank, 0] = q_ref[sources[rank]]
+            send_qg[rank, 1] = g_ref[sources[rank]]
+        send(send_qg.at[stage * inner + inner - 1 - mx], in_qg.at[stage, :, tile(mx, rows), :],
+             sem_send.at[1], sem_qg.at[stage], partner)
+        if stage > 0:
+            send_keys(stage)
+        in_qg[stage, :, tile(mx, rows), :] = send_qg[stage * inner + mx]
+        in_kv[stage, own_rows, :] = send_kv[stage * inner + mx]
+    in_p[tile(me, slot), :] = send_p[...]
+
+    keys_total = total + n * slot
+    row_id = lax.broadcasted_iota(jnp.int32, (stacked, keys_total), 0)
+    position = mz * block + row_id - (row_id // block) * block
+    col_id = lax.broadcasted_iota(jnp.int32, (stacked, keys_total), 1)
+    in_prompt = col_id - total
+    prompt_slot = in_prompt // slot
+    prompt_row = in_prompt - prompt_slot * slot
+    prompt_id = prompt_slot * prompt_rows + prompt_row
+    far = jnp.int32(2**30)
+    prompt_rank = jnp.where(prompt_row < prompt_rows, prompt_id, far)
+    ahead = col_id - position
+    live_row = lax.broadcasted_iota(jnp.int32, (stacked, HEAD_DIM), 0)
+    live_position = mz * block + live_row - (live_row // block) * block
+
+    wait_bytes(in_p.at[0 : (n - 1) * slot, :], sem_p)
+    acc[...] = jnp.zeros_like(acc)
+    for stage in range(outer):
+        home = stage * inner + mx
+        source = resident(home)
+        length = len_ref[source]
+        visible = seen_ref[source]
+        allowed = jnp.where(col_id < total, ahead, prompt_rank - visible + 1) <= 0
+        live = live_position < length
+        for step in range(outer):
+            @pl.when(step < mz)
+            def _():
+                wait_bytes(in_kv.at[stage, 0:block, :], sem_kv.at[stage, step])
+
+            @pl.when(step == mz)
+            def _():
+                wait_bytes(in_kv.at[stage, 0:rows, :], sem_kv.at[stage, step])
+        wait_bytes(in_qg.at[stage, :, 0:rows, :], sem_qg.at[stage])
+        for h in range(kv_heads):
+            kc, vc = pair_cols(h)
+            keys = jnp.concatenate(
+                [in_kv[stage, :, kc : kc + HEAD_DIM], in_p[:, kc : kc + HEAD_DIM]], axis=0
+            )
+            values = jnp.concatenate(
+                [in_kv[stage, :, vc : vc + HEAD_DIM], in_p[:, vc : vc + HEAD_DIM]], axis=0
+            )
+            heads = [
+                slice((h * group + a) * HEAD_DIM, (h * group + a + 1) * HEAD_DIM)
+                for a in range(group)
+            ]
+            query = jnp.concatenate([in_qg[stage, 0, :, c] for c in heads], axis=0)
+            grad = jnp.concatenate([in_qg[stage, 1, :, c] for c in heads], axis=0)
+            grad_wide = jnp.where(live, grad.astype(jnp.float32), 0.0)
+            grad = grad_wide.astype(jnp.bfloat16)
+            logits = jnp.where(allowed, dot_last(query, keys) * scale, NEG_FILL)
+            exped = jnp.exp(logits - jnp.max(logits, axis=1, keepdims=True))
+            prob = exped * (1.0 / jnp.sum(exped, axis=1, keepdims=True))
+            weights = prob.astype(jnp.bfloat16)
+            output = jnp.where(live, dot_plain(weights, values), 0.0).astype(jnp.bfloat16)
+            row_dot = jnp.sum(grad_wide * output.astype(jnp.float32), axis=1, keepdims=True)
+            dlogit = (prob * (dot_last(grad, values) - row_dot)).astype(jnp.bfloat16)
+            dquery = (dot_plain(dlogit, keys) * scale).astype(jnp.bfloat16)
+            for a in range(group):
+                part = slice(a * block, (a + 1) * block)
+                out_send[stage, :, heads[a]] = output[part]
+                grad_q[stage, :, heads[a]] = dquery[part]
+            dkey = dot_first(dlogit, query) * scale
+            dvalue = dot_first(weights, grad)
+            for col, part in ((kc, dkey), (vc, dvalue)):
+                grad_kv[stage, :, col : col + HEAD_DIM] = part[:total].astype(jnp.bfloat16)
+                acc[:, col : col + HEAD_DIM] += part[total:]
+
+        @pl.when(mz != stage)
+        def _():
+            send(out_send.at[stage], out_ref.at[0, tile(mz, block), :],
+                 sem_send.at[2], sem_out, home)
+
+        @pl.when(mz == stage)
+        def _():
+            pltpu.make_async_copy(
+                out_send.at[stage], out_ref.at[0, tile(mz, block), :], sem_local.at[0]
+            ).start()
+
+        for step in range(outer):
+            @pl.when(mz - step >= 0)
+            def _():
+                for dx in range(inner):
+                    chunk = (mz - step) * inner + dx
+
+                    def go():
+                        send(grad_kv.at[stage, tile(chunk, rows), :], back_kv.at[mz, home],
+                             sem_grad_out.at[step], sem_grad.at[mz], chunk)
+
+                    if step == 0:
+                        pl.when(mx != dx)(go)
+                    else:
+                        go()
+        send(grad_q.at[stage, tile(inner - 1 - mx, rows), :], back_q.at[home],
+             sem_send.at[3], sem_q, partner)
+        pltpu.make_async_copy(
+            grad_q.at[stage, tile(mx, rows), :], back_q.at[home], sem_local.at[1]
+        ).start()
+        back_kv[mz, home] = grad_kv[stage, own_rows, :]
+    grad_p[...] = acc[...].astype(jnp.bfloat16)
+    for step in range(1, n):
+        peer = lax.rem(me + step, n)
+        send(grad_p.at[tile(peer, slot), :], back_p.at[me], sem_send.at[4], sem_gp, peer)
+    back_p[me] = grad_p[tile(me, slot), :]
+
+    for step in range(outer):
+        @pl.when(step > mz)
+        def _():
+            wait_bytes(back_kv.at[step], sem_grad.at[step])
+
+        @pl.when(step == mz)
+        def _():
+            wait_bytes(back_kv.at[step, 0:outer], sem_grad.at[step])
+    for r in range(n):
+        home = home_ref[r]
+        summed = back_kv[0, home].astype(jnp.float32)
+        for step in range(1, outer):
+            summed = summed + back_kv[step, home].astype(jnp.float32)
+        summed = summed.astype(jnp.bfloat16)
+        for h in range(kv_heads):
+            kc, vc = pair_cols(h)
+            own = slice(h * HEAD_DIM, (h + 1) * HEAD_DIM)
+            dk_ref[r, :, own] = summed[:, kc : kc + HEAD_DIM]
+            dv_ref[r, :, own] = summed[:, vc : vc + HEAD_DIM]
+    wait_bytes(back_p.at[0 : n - 1], sem_gp)
+    prompt_sum = back_p[0].astype(jnp.float32)
+    for rank in range(1, n):
+        prompt_sum = prompt_sum + back_p[rank].astype(jnp.float32)
+    for h in range(kv_heads):
+        kc, vc = pair_cols(h)
+        own = slice(h * HEAD_DIM, (h + 1) * HEAD_DIM)
+        dpk_ref[:, own] = prompt_sum[:prompt_rows, kc : kc + HEAD_DIM].astype(jnp.bfloat16)
+        dpv_ref[:, own] = prompt_sum[:prompt_rows, vc : vc + HEAD_DIM].astype(jnp.bfloat16)
+
+    wait_bytes(out_send.at[0], sem_local.at[0])
+    wait_bytes(back_q.at[0:outer], sem_local.at[1])
+    wait_bytes(out_send.at[0 : outer - 1], sem_out)
+    wait_bytes(back_q.at[0:outer], sem_q)
+    wait_bytes(back_p.at[0 : n - 1], sem_send.at[0])
+    wait_bytes(in_qg.at[:, :, 0:rows, :], sem_send.at[1])
+    wait_bytes(out_send.at[0 : outer - 1], sem_send.at[2])
+    wait_bytes(back_q.at[0:outer], sem_send.at[3])
+    wait_bytes(back_p.at[0 : n - 1], sem_send.at[4])
+    for sem in (sem_kv_out, sem_grad_out):
+        for step in range(outer):
+            reached = mz + step < outer if sem is sem_kv_out else mz - step >= 0
+
+            @pl.when(reached)
+            def _():
+                wait_bytes(send_kv.at[0 : outer if step == 0 else n], sem.at[step])
+
+
+def place_kernel(
+    n, out_in, back_q, dk_in, dv_in, dpk_in, dpv_in, home_hbm,
+    out_ref, dq_ref, dk_ref, dv_ref, dpk_ref, dpv_ref, home_ref, sems, sem_row, sem_home,
+):
+    ranks = pltpu.make_async_copy(home_hbm, home_ref, sem_home)
+    ranks.start()
+    pairs = ((out_in, out_ref), (dk_in, dk_ref), (dv_in, dv_ref), (dpk_in, dpk_ref), (dpv_in, dpv_ref))
+    copies = [pltpu.make_async_copy(src, dst, sems.at[i]) for i, (src, dst) in enumerate(pairs)]
+    for copy in copies:
+        copy.start()
+    ranks.wait()
+    moves = [
+        pltpu.make_async_copy(back_q.at[home_ref[r]], dq_ref.at[r], sem_row.at[r]) for r in range(n)
+    ]
+    for copy in moves:
+        copy.start()
+    for copy in copies + moves:
+        copy.wait()
+
+
+def kernel_body(*arrays):
+    query, key, _, _, prompt_key, _, lengths, home_rank, _ = arrays
+    n = lax.axis_size("seq")
+    inner = 2
+    outer = n // inner
+    rows, width = query.shape[1:]
+    kv_width = key.shape[2]
+    prompt_rows = prompt_key.shape[0]
+    slot = -(-prompt_rows // ROW_TILE) * ROW_TILE
+    total = n * rows
+    bf16 = jnp.bfloat16
+    vmem = pl.BlockSpec(memory_space=pltpu.VMEM)
+    hbm = pl.BlockSpec(memory_space=pltpu.HBM)
+    shapes = (
+        jax.ShapeDtypeStruct((1, total, width), bf16),
+        jax.ShapeDtypeStruct(query.shape, bf16),
+        jax.ShapeDtypeStruct(key.shape, bf16),
+        jax.ShapeDtypeStruct(key.shape, bf16),
+        jax.ShapeDtypeStruct(prompt_key.shape, bf16),
+        jax.ShapeDtypeStruct(prompt_key.shape, bf16),
+    )
+    dma = pltpu.SemaphoreType.DMA
+    results = pl.pallas_call(
+        functools.partial(kernel, n, inner, prompt_rows),
+        out_shape=shapes,
+        in_specs=[hbm] * 4 + [vmem] * 2 + [hbm] * 3,
+        out_specs=(hbm,) * 2 + (vmem,) * 4,
+        scratch_shapes=[
+            pltpu.VMEM(query.shape, bf16),
+            pltpu.VMEM(key.shape, bf16),
+            pltpu.VMEM(key.shape, bf16),
+            pltpu.VMEM(query.shape, bf16),
+            pltpu.SMEM(lengths.shape, jnp.int32),
+            pltpu.SMEM(lengths.shape, jnp.int32),
+            pltpu.SMEM(lengths.shape, jnp.int32),
+            pltpu.VMEM((n, 2, rows, width), bf16),
+            pltpu.VMEM((n, rows, 2 * kv_width), bf16),
+            pltpu.VMEM((slot, 2 * kv_width), bf16),
+            pltpu.VMEM((outer, 2, inner * rows, width), bf16),
+            pltpu.VMEM((outer, total, 2 * kv_width), bf16),
+            pltpu.VMEM((n * slot, 2 * kv_width), bf16),
+            pltpu.VMEM((outer, inner * rows, width), bf16),
+            pltpu.VMEM((outer, inner * rows, width), bf16),
+            pltpu.VMEM((outer, total, 2 * kv_width), bf16),
+            pltpu.VMEM((n * slot, 2 * kv_width), bf16),
+            pltpu.VMEM((outer, n, rows, 2 * kv_width), bf16),
+            pltpu.VMEM((n, slot, 2 * kv_width), bf16),
+            pltpu.VMEM((n * slot, 2 * kv_width), jnp.float32),
+            dma((7,)), dma((2,)), dma((5,)), dma((outer,)), dma((outer,)),
+            dma, dma((outer,)), dma((outer, outer)), dma, dma, dma((outer,)), dma,
+        ],
+        compiler_params=pltpu.CompilerParams(
+            collective_id=0, has_side_effects=True, vmem_limit_bytes=48 * 1024 * 1024
+        ),
+    )(*arrays)
+    return pl.pallas_call(
+        functools.partial(place_kernel, n),
+        out_shape=shapes,
+        in_specs=[hbm] * 7,
+        out_specs=(hbm,) * 6,
+        scratch_shapes=[pltpu.SMEM(home_rank.shape, jnp.int32), dma((5,)), dma((n,)), dma],
+    )(*results, home_rank)
+
+
+def body(*arrays):
+    rows = arrays[0].shape[1]
+    slot = -(-arrays[4].shape[0] // ROW_TILE) * ROW_TILE
+    if rows % ROW_TILE == 0 and slot == rows and lax.axis_size("seq") % 2 == 0:
+        return kernel_body(*arrays)
+    return collective_body(*arrays)
+
+
 def solution(mesh):
     placed = (
         P("group", "seq", "head"),

time: 198 us -> 90.4 us (0.46)
  blocking collectives: 85.2 us -> 0 us
  Pallas kernels: 0 us -> 78.2 us
  starting transfers between devices: 41.6 us -> 0 us
  waiting for transfers between devices: 30 us -> 0 us
  local copies, waits for them, and re-layouts: 22.9 us -> 11.1 us
  other arithmetic: 9.71 us -> 0 us
  matrix products: 3.45 us -> 0 us
  between operations: 3.84 us -> 0.67 us
    pallas_call x0 -> x2, Pallas kernels: none -> 78.2 us  [the longest x1 40.8 us: kernel_body(): pl.pallas_call(functools.partial(kernel, n, inner, prompt_rows), out_shap...]
    all_gather x2 -> x0, blocking collectives: 61.8 us -> none  [the longest x1 31.2 us: body(): lax.all_gather(prompt_key, 'seq', axis=0, tiled=True)]
    all_to_all x7 -> x0, starting transfers between devices: 32.3 us -> none  [the longest x1 7.38 us: body(): lax.all_to_all(response_grad[resident], 'seq', split_axis=0, concat_axis=...]
    all_to_all x7 -> x0, waiting for transfers between devices: 30 us -> none  [the longest x1 13.1 us: body(): lax.all_to_all(response_grad[resident], 'seq', split_axis=0, concat_axis=...]
    unnamed x1 -> x0, blocking collectives: 23.4 us -> none
    unnamed x4 -> x0, starting transfers between devices: 9.32 us -> none
    gather x7 -> x0, local copies, waits for them, and re-layouts: 8.83 us -> none  [the longest x1 1.37 us: body(): response_query[resident]]
    unnamed x6 -> x0, other arithmetic: 6.82 us -> none
  transfers between devices with their start and end apart: 11 -> 0, of which waited for: 5 -> 0; matrix products, arithmetic and copies ran while one was open for 24% -> 0% of each run, Pallas kernels for 0% -> 0%
where the time goes in v2:
time: 90.4 us; the launch traced here: 90 us
  Pallas kernels  78.2 us (87%)
  local copies, waits for them, and re-layouts  11.1 us (12%)
    pallas_call x1, Pallas kernels, kernel_body(): pl.pallas_call(functools.partial(kernel, n, inner, prompt_rows), out_shap...  40.8 us
    pallas_call x1, Pallas kernels, kernel_body(): pl.pallas_call(functools.partial(place_kernel, n), out_shape=shapes, in_s...  37.5 us
    unnamed x30, local copies, waits for them, and re-layouts  11.1 us

profile of v2, /device:TPU:0, one launch (start us, length us, event | category | flops | bytes accessed | tf_op | source)
XLA Modules:
  0.0 90.0 jit_solution(18017121436385164984)
XLA Ops:
  0.6 0.0 copy-start
  0.6 1.0 %copy-done = bf16[8,16,2048]{2,1,0:T(8,128)(2,1)S(1)} copy-done((bf16[8,16,2048]{2,1,0:T(8,128)(2,1)S(1)}, bf16[8,16,2048]{2,1,0:T(8,128)(2,1)}, u32[]{:S(2)}) %copy-start) | copy-done | bytes 524312
  1.7 0.0 copy-start.1
  1.7 1.0 %copy-done.1 = bf16[8,16,2048]{2,1,0:T(8,128)(2,1)S(1)} copy-done((bf16[8,16,2048]{2,1,0:T(8,128)(2,1)S(1)}, bf16[8,16,2048]{2,1,0:T(8,128)(2,1)}, u32[]{:S(2)}) %copy-start.1) | copy-done | bytes 524312
  2.7 0.0 copy-start.4
  2.7 0.8 copy-done.4
  3.6 0.0 copy-start.5
  3.6 0.8 copy-done.5
  4.4 0.0 copy-start.8
  4.4 0.7 copy-done.8
  5.1 0.0 copy-start.9
  5.1 0.7 copy-done.9
  5.8 0.7 copy-done.12
  6.5 0.7 copy-done.13
  7.1 0.7 copy-done.14
  7.8 40.8 %shard_map.136 = (bf16[1,128,2048]{2,1,0:T(8,128)(2,1)S(1)}, bf16[8,16,2048]{2,1,0:T(8,128)(2,1)S(1)}, bf16[8,16,256]{2,1,0:T(8,128)(2,1)S(1)}, bf16[8,16,256]{2...) custom-call(bf16[8,16,2048]{2,1,0:T(8,128)(2,1)S(1)} %copy-done, ...), custom_call_target="tpu_custom_call" | custom-call | tf_op jit(solution)/shard_map/pallas_call | solution.py:528
  48.5 0.0 copy-start.2
  48.6 0.8 copy-done.2
  49.3 0.8 copy-done.3
  50.1 0.6 copy-done.6
  50.7 0.6 copy-done.7
  51.4 0.6 copy-done.10
  52.0 0.6 copy-done.11
  52.5 37.5 %shard_map.137 = (bf16[1,128,2048]{2,1,0:T(8,128)(2,1)}, bf16[8,16,2048]{2,1,0:T(8,128)(2,1)}, bf16[8,16,256]{2,1,0:T(8,128)(2,1)}, bf16[8,16,256]{2,1,0:T(8,128...) custom-call(bf16[1,128,2048]{2,1,0:T(8,128)(2,1)} %copy-done.2, bf16[8,16,2048]{2,1,0:T(8,128)(2,1)} %copy-done.3, ...), custom_call_target="tpu_custom_call" | custom-call | tf_op jit(solution)/shard_map/pallas_call | solution.py:561
  (8 shorter events, 0.0 us)
Async XLA Ops:
  0.6 1.0 %copy-start = (bf16[8,16,2048]{2,1,0:T(8,128)(2,1)S(1)}, bf16[8,16,2048]{2,1,0:T(8,128)(2,1)}, u32[]{:S(2)}) copy-start(bf16[8,16,2048]{2,1,0:T(8,128)(2,1)} %q_hbm.1) | copy-start | bytes 1572868
  1.7 1.0 %copy-start.1 = (bf16[8,16,2048]{2,1,0:T(8,128)(2,1)S(1)}, bf16[8,16,2048]{2,1,0:T(8,128)(2,1)}, u32[]{:S(2)}) copy-start(bf16[8,16,2048]{2,1,0:T(8,128)(2,1)} %g_hbm.1) | copy-start | bytes 1572868
  2.7 0.8 copy-start.4
  3.6 0.8 copy-start.5
  4.4 0.7 copy-start.8
  5.1 0.7 copy-start.9
  5.8 0.7 copy-start.12
  6.5 0.7 copy-start.13
  7.1 0.7 copy-start.14
  48.5 0.8 copy-start.2
  49.3 0.8 copy-start.3
  50.1 0.6 copy-start.6
  50.7 0.6 copy-start.7
  51.4 0.6 copy-start.10
  52.0 0.6 copy-start.11

commit v3 on v2

--- a/solution.py
+++ b/solution.py
@@ -195,6 +195,7 @@
 
 
 ROW_TILE = 16
+VMEM_BYTES = 64 * 1024 * 1024 - 256 * 1024
 MESH = pl.DeviceIdType.MESH
 
 
@@ -216,9 +217,10 @@
 
 def kernel(
     n, inner, prompt_rows,
-    q_hbm, k_hbm, v_hbm, g_hbm, pk_ref, pv_ref, len_hbm, home_hbm, seen_hbm,
-    out_ref, back_q, dk_ref, dv_ref, dpk_ref, dpv_ref,
+    q_hbm, k_hbm, v_hbm, g_hbm, pk_hbm, pv_hbm, len_hbm, home_hbm, seen_hbm,
+    out_ref, back_q, dk_hbm, dv_hbm, dpk_hbm, dpv_hbm,
     q_ref, k_ref, v_ref, g_ref, len_ref, home_ref, seen_ref,
+    pk_ref, pv_ref, dk_ref, dv_ref, dpk_ref, dpv_ref,
     send_qg, send_kv, send_p, in_qg, in_kv, in_p,
     out_send, grad_q, grad_kv, grad_p, back_kv, back_p, acc,
     sem_load, sem_local, sem_send, sem_kv_out, sem_grad_out,
@@ -241,7 +243,8 @@
         pltpu.make_async_copy(src, dst, sem_load.at[i])
         for i, (src, dst) in enumerate((
             (len_hbm, len_ref), (home_hbm, home_ref), (seen_hbm, seen_ref),
-            (k_hbm, k_ref), (v_hbm, v_ref), (q_hbm, q_ref), (g_hbm, g_ref),
+            (k_hbm, k_ref), (v_hbm, v_ref), (pk_hbm, pk_ref), (pv_hbm, pv_ref),
+            (q_hbm, q_ref), (g_hbm, g_ref),
         ))
     ]
     for load in loads:
@@ -266,6 +269,8 @@
     def pair_cols(head):
         return head * 2 * HEAD_DIM, head * 2 * HEAD_DIM + HEAD_DIM
 
+    for load in loads[:7]:
+        load.wait()
     prompt_pad = jnp.zeros((slot - prompt_rows, HEAD_DIM), jnp.float32)
     for h in range(kv_heads):
         kc, vc = pair_cols(h)
@@ -275,8 +280,6 @@
             if slot > prompt_rows:
                 part = jnp.concatenate([part, prompt_pad], axis=0)
             send_p[:, col : col + HEAD_DIM] = part.astype(jnp.bfloat16)
-    for load in loads[:5]:
-        load.wait()
 
     def resident(rank):
         found = jnp.int32(0)
@@ -318,8 +321,8 @@
     send_keys(0)
     for step in range(1, n):
         send(send_p, in_p.at[tile(me, slot), :], sem_send.at[0], sem_p, lax.rem(me + step, n))
-    loads[5].wait()
-    loads[6].wait()
+    loads[7].wait()
+    loads[8].wait()
     for stage in range(outer):
         for dx in range(inner):
             rank = stage * inner + dx
@@ -465,6 +468,14 @@
         dpk_ref[:, own] = prompt_sum[:prompt_rows, kc : kc + HEAD_DIM].astype(jnp.bfloat16)
         dpv_ref[:, own] = prompt_sum[:prompt_rows, vc : vc + HEAD_DIM].astype(jnp.bfloat16)
 
+    stores = [
+        pltpu.make_async_copy(src, dst, sem_load.at[i])
+        for i, (src, dst) in enumerate((
+            (dk_ref, dk_hbm), (dv_ref, dv_hbm), (dpk_ref, dpk_hbm), (dpv_ref, dpv_hbm),
+        ))
+    ]
+    for store in stores:
+        store.start()
     wait_bytes(out_send.at[0], sem_local.at[0])
     wait_bytes(back_q.at[0:outer], sem_local.at[1])
     wait_bytes(out_send.at[0 : outer - 1], sem_out)
@@ -481,25 +492,32 @@
             @pl.when(reached)
             def _():
                 wait_bytes(send_kv.at[0 : outer if step == 0 else n], sem.at[step])
-
-
-def place_kernel(
-    n, out_in, back_q, dk_in, dv_in, dpk_in, dpv_in, home_hbm,
-    out_ref, dq_ref, dk_ref, dv_ref, dpk_ref, dpv_ref, home_ref, sems, sem_row, sem_home,
-):
+    for store in stores:
+        store.wait()
+
+
+def place_kernel(n, *refs):
+    sources, home_hbm = refs[:6], refs[6]
+    results, held, home_ref = refs[7:13], refs[13:19], refs[19]
+    sem_in, sem_out, sem_row, sem_home = refs[20:]
     ranks = pltpu.make_async_copy(home_hbm, home_ref, sem_home)
     ranks.start()
-    pairs = ((out_in, out_ref), (dk_in, dk_ref), (dv_in, dv_ref), (dpk_in, dpk_ref), (dpv_in, dpv_ref))
-    copies = [pltpu.make_async_copy(src, dst, sems.at[i]) for i, (src, dst) in enumerate(pairs)]
-    for copy in copies:
+    reads = [
+        pltpu.make_async_copy(src, dst, sem_in.at[i]) for i, (src, dst) in enumerate(zip(sources, held))
+    ]
+    for copy in reads:
         copy.start()
+    writes = []
+    for i in (0, 2, 3, 4, 5):
+        reads[i].wait()
+        writes.append(pltpu.make_async_copy(held[i], results[i], sem_out.at[i]))
+        writes[-1].start()
+    reads[1].wait()
     ranks.wait()
-    moves = [
-        pltpu.make_async_copy(back_q.at[home_ref[r]], dq_ref.at[r], sem_row.at[r]) for r in range(n)
-    ]
-    for copy in moves:
-        copy.start()
-    for copy in copies + moves:
+    for r in range(n):
+        writes.append(pltpu.make_async_copy(held[1].at[home_ref[r]], results[1].at[r], sem_row.at[r]))
+        writes[-1].start()
+    for copy in writes:
         copy.wait()
 
 
@@ -514,7 +532,6 @@
     slot = -(-prompt_rows // ROW_TILE) * ROW_TILE
     total = n * rows
     bf16 = jnp.bfloat16
-    vmem = pl.BlockSpec(memory_space=pltpu.VMEM)
     hbm = pl.BlockSpec(memory_space=pltpu.HBM)
     shapes = (
         jax.ShapeDtypeStruct((1, total, width), bf16),
@@ -528,8 +545,8 @@
     results = pl.pallas_call(
         functools.partial(kernel, n, inner, prompt_rows),
         out_shape=shapes,
-        in_specs=[hbm] * 4 + [vmem] * 2 + [hbm] * 3,
-        out_specs=(hbm,) * 2 + (vmem,) * 4,
+        in_specs=[hbm] * 9,
+        out_specs=(hbm,) * 6,
         scratch_shapes=[
             pltpu.VMEM(query.shape, bf16),
             pltpu.VMEM(key.shape, bf16),
@@ -538,6 +555,9 @@
             pltpu.SMEM(lengths.shape, jnp.int32),
             pltpu.SMEM(lengths.shape, jnp.int32),
             pltpu.SMEM(lengths.shape, jnp.int32),
+            pltpu.VMEM(prompt_key.shape, bf16),
+            pltpu.VMEM(prompt_key.shape, bf16),
+            *(pltpu.VMEM(shape.shape, bf16) for shape in shapes[2:]),
             pltpu.VMEM((n, 2, rows, width), bf16),
             pltpu.VMEM((n, rows, 2 * kv_width), bf16),
             pltpu.VMEM((slot, 2 * kv_width), bf16),
@@ -551,11 +571,11 @@
             pltpu.VMEM((outer, n, rows, 2 * kv_width), bf16),
             pltpu.VMEM((n, slot, 2 * kv_width), bf16),
             pltpu.VMEM((n * slot, 2 * kv_width), jnp.float32),
-            dma((7,)), dma((2,)), dma((5,)), dma((outer,)), dma((outer,)),
+            dma((9,)), dma((2,)), dma((5,)), dma((outer,)), dma((outer,)),
             dma, dma((outer,)), dma((outer, outer)), dma, dma, dma((outer,)), dma,
         ],
         compiler_params=pltpu.CompilerParams(
-            collective_id=0, has_side_effects=True, vmem_limit_bytes=48 * 1024 * 1024
+            collective_id=0, has_side_effects=True, vmem_limit_bytes=VMEM_BYTES
         ),
     )(*arrays)
     return pl.pallas_call(
@@ -563,7 +583,12 @@
         out_shape=shapes,
         in_specs=[hbm] * 7,
         out_specs=(hbm,) * 6,
-        scratch_shapes=[pltpu.SMEM(home_rank.shape, jnp.int32), dma((5,)), dma((n,)), dma],
+        scratch_shapes=[
+            *(pltpu.VMEM(shape.shape, bf16) for shape in shapes),
+            pltpu.SMEM(home_rank.shape, jnp.int32),
+            dma((6,)), dma((6,)), dma((n,)), dma,
+        ],
+        compiler_params=pltpu.CompilerParams(vmem_limit_bytes=VMEM_BYTES),
     )(*results, home_rank)
 
 

time: 90.4 us -> 44.3 us (0.49)
  Pallas kernels: 78.2 us -> 43.4 us
  local copies, waits for them, and re-layouts: 11.1 us -> 0 us
    pallas_call x1, Pallas kernels: 37.5 us -> 2.23 us  [kernel_body(): pl.pallas_call(functools.partial(place_kernel, n), out_shape=shapes, in_s...]
    unnamed x30 -> x0, local copies, waits for them, and re-layouts: 11.1 us -> none
where the time goes in v3:
time: 44.3 us; the launch traced here: 44.1 us
  Pallas kernels  43.4 us (98%)
  between operations  0.64 us (1%)
    pallas_call x1, Pallas kernels, kernel_body(): pl.pallas_call(functools.partial(kernel, n, inner, prompt_rows), out_shap...  41.2 us
    pallas_call x1, Pallas kernels, kernel_body(): pl.pallas_call(functools.partial(place_kernel, n), out_shape=shapes, in_s...  2.23 us

profile of v3, /device:TPU:0, one launch (start us, length us, event | category | flops | bytes accessed | tf_op | source)
XLA Modules:
  0.0 44.1 jit_solution(1634264257579838056)
XLA Ops:
  0.6 41.2 %shard_map.136 = (bf16[1,128,2048]{2,1,0:T(8,128)(2,1)}, bf16[8,16,2048]{2,1,0:T(8,128)(2,1)}, bf16[8,16,256]{2,1,0:T(8,128)(2,1)}, bf16[8,16,256]{2,1,0:T(8,128...) custom-call(bf16[8,16,2048]{2,1,0:T(8,128)(2,1)} %q_hbm.1, bf16[8,16,256]{2,1,0:T(8,128)(2,1)} %k_hbm.1, ...), custom_call_target="tpu_custom_call" | custom-call | tf_op jit(solution)/shard_map/pallas_call | solution.py:545
  41.9 2.2 %shard_map.137 = (bf16[1,128,2048]{2,1,0:T(8,128)(2,1)}, bf16[8,16,2048]{2,1,0:T(8,128)(2,1)}, bf16[8,16,256]{2,1,0:T(8,128)(2,1)}, bf16[8,16,256]{2,1,0:T(8,128...) custom-call(bf16[1,128,2048]{2,1,0:T(8,128)(2,1)} %get-tuple-element.12.refs_0_, ...), custom_call_target="tpu_custom_call" | custom-call | tf_op jit(solution)/shard_map/pallas_call | solution.py:581

commit v4 on v3

--- a/solution.py
+++ b/solution.py
@@ -318,6 +318,17 @@
                     else:
                         go()
 
+    head_width = group * HEAD_DIM
+
+    def send_rows(unit):
+        stage, h = unit // kv_heads, unit % kv_heads
+        cols = pl.ds(h * head_width, head_width)
+        send(send_qg.at[stage * inner + inner - 1 - mx, :, :, cols],
+             in_qg.at[stage, :, tile(mx, rows), cols],
+             sem_send.at[1], sem_qg.at[unit], partner)
+
+    units = outer * kv_heads
+    lead = 2
     send_keys(0)
     for step in range(1, n):
         send(send_p, in_p.at[tile(me, slot), :], sem_send.at[0], sem_p, lax.rem(me + step, n))
@@ -328,10 +339,9 @@
             rank = stage * inner + dx
             send_qg[rank, 0] = q_ref[sources[rank]]
             send_qg[rank, 1] = g_ref[sources[rank]]
-        send(send_qg.at[stage * inner + inner - 1 - mx], in_qg.at[stage, :, tile(mx, rows), :],
-             sem_send.at[1], sem_qg.at[stage], partner)
-        if stage > 0:
-            send_keys(stage)
+        for unit in range(stage * kv_heads, (stage + 1) * kv_heads):
+            if unit < lead:
+                send_rows(unit)
         in_qg[stage, :, tile(mx, rows), :] = send_qg[stage * inner + mx]
         in_kv[stage, own_rows, :] = send_kv[stage * inner + mx]
     in_p[tile(me, slot), :] = send_p[...]
@@ -367,8 +377,14 @@
             @pl.when(step == mz)
             def _():
                 wait_bytes(in_kv.at[stage, 0:rows, :], sem_kv.at[stage, step])
-        wait_bytes(in_qg.at[stage, :, 0:rows, :], sem_qg.at[stage])
+        if stage + 1 < outer:
+            send_keys(stage + 1)
         for h in range(kv_heads):
+            unit = stage * kv_heads + h
+            cols = pl.ds(h * head_width, head_width)
+            wait_bytes(in_qg.at[stage, :, 0:rows, cols], sem_qg.at[unit])
+            if unit + lead < units:
+                send_rows(unit + lead)
             kc, vc = pair_cols(h)
             keys = jnp.concatenate(
                 [in_kv[stage, :, kc : kc + HEAD_DIM], in_p[:, kc : kc + HEAD_DIM]], axis=0
@@ -402,15 +418,21 @@
                 grad_kv[stage, :, col : col + HEAD_DIM] = part[:total].astype(jnp.bfloat16)
                 acc[:, col : col + HEAD_DIM] += part[total:]
 
-        @pl.when(mz != stage)
-        def _():
-            send(out_send.at[stage], out_ref.at[0, tile(mz, block), :],
-                 sem_send.at[2], sem_out, home)
-
-        @pl.when(mz == stage)
-        def _():
+            @pl.when(mz != stage)
+            def _():
+                send(out_send.at[stage, :, cols], out_ref.at[0, tile(mz, block), cols],
+                     sem_send.at[2], sem_out, home)
+
+            @pl.when(mz == stage)
+            def _():
+                pltpu.make_async_copy(
+                    out_send.at[stage, :, cols], out_ref.at[0, tile(mz, block), cols], sem_local.at[0]
+                ).start()
+
+            send(grad_q.at[stage, tile(inner - 1 - mx, rows), cols], back_q.at[home, :, cols],
+                 sem_send.at[3], sem_q, partner)
             pltpu.make_async_copy(
-                out_send.at[stage], out_ref.at[0, tile(mz, block), :], sem_local.at[0]
+                grad_q.at[stage, tile(mx, rows), cols], back_q.at[home, :, cols], sem_local.at[1]
             ).start()
 
         for step in range(outer):
@@ -427,11 +449,6 @@
                         pl.when(mx != dx)(go)
                     else:
                         go()
-        send(grad_q.at[stage, tile(inner - 1 - mx, rows), :], back_q.at[home],
-             sem_send.at[3], sem_q, partner)
-        pltpu.make_async_copy(
-            grad_q.at[stage, tile(mx, rows), :], back_q.at[home], sem_local.at[1]
-        ).start()
         back_kv[mz, home] = grad_kv[stage, own_rows, :]
     grad_p[...] = acc[...].astype(jnp.bfloat16)
     for step in range(1, n):
@@ -572,7 +589,7 @@
             pltpu.VMEM((n, slot, 2 * kv_width), bf16),
             pltpu.VMEM((n * slot, 2 * kv_width), jnp.float32),
             dma((9,)), dma((2,)), dma((5,)), dma((outer,)), dma((outer,)),
-            dma, dma((outer,)), dma((outer, outer)), dma, dma, dma((outer,)), dma,
+            dma, dma((outer * (kv_width // HEAD_DIM),)), dma((outer, outer)), dma, dma, dma((outer,)), dma,
         ],
         compiler_params=pltpu.CompilerParams(
             collective_id=0, has_side_effects=True, vmem_limit_bytes=VMEM_BYTES

time: 44.3 us -> 43.8 us (0.989)
    pallas_call x1, Pallas kernels: 41.2 us -> 40.7 us  [kernel_body(): pl.pallas_call(functools.partial(kernel, n, inner, prompt_rows), out_shap...]
where the time goes in v4:
time: 43.8 us; the launch traced here: 43.6 us
  Pallas kernels  43 us (98%)
  between operations  0.64 us (1%)
    pallas_call x1, Pallas kernels, kernel_body(): pl.pallas_call(functools.partial(kernel, n, inner, prompt_rows), out_shap...  40.7 us
    pallas_call x1, Pallas kernels, kernel_body(): pl.pallas_call(functools.partial(place_kernel, n), out_shape=shapes, in_s...  2.23 us

profile of v4, /device:TPU:0, one launch (start us, length us, event | category | flops | bytes accessed | tf_op | source)
XLA Modules:
  0.0 43.6 jit_solution(14777837540503791380)
XLA Ops:
  0.6 40.7 %shard_map.136 = (bf16[1,128,2048]{2,1,0:T(8,128)(2,1)}, bf16[8,16,2048]{2,1,0:T(8,128)(2,1)}, bf16[8,16,256]{2,1,0:T(8,128)(2,1)}, bf16[8,16,256]{2,1,0:T(8,128...) custom-call(bf16[8,16,2048]{2,1,0:T(8,128)(2,1)} %q_hbm.1, bf16[8,16,256]{2,1,0:T(8,128)(2,1)} %k_hbm.1, ...), custom_call_target="tpu_custom_call" | custom-call | tf_op jit(solution)/shard_map/pallas_call | solution.py:562
  41.4 2.2 %shard_map.137 = (bf16[1,128,2048]{2,1,0:T(8,128)(2,1)}, bf16[8,16,2048]{2,1,0:T(8,128)(2,1)}, bf16[8,16,256]{2,1,0:T(8,128)(2,1)}, bf16[8,16,256]{2,1,0:T(8,128...) custom-call(bf16[1,128,2048]{2,1,0:T(8,128)(2,1)} %get-tuple-element.12.refs_0_, ...), custom_call_target="tpu_custom_call" | custom-call | tf_op jit(solution)/shard_map/pallas_call | solution.py:598

commit v5 on v4

--- a/solution.py
+++ b/solution.py
@@ -195,6 +195,7 @@
 
 
 ROW_TILE = 16
+LOG2E = 1.4426950408889634
 VMEM_BYTES = 64 * 1024 * 1024 - 256 * 1024
 MESH = pl.DeviceIdType.MESH
 
@@ -347,9 +348,8 @@
     in_p[tile(me, slot), :] = send_p[...]
 
     keys_total = total + n * slot
-    row_id = lax.broadcasted_iota(jnp.int32, (stacked, keys_total), 0)
-    position = mz * block + row_id - (row_id // block) * block
-    col_id = lax.broadcasted_iota(jnp.int32, (stacked, keys_total), 1)
+    position = mz * block + lax.broadcasted_iota(jnp.int32, (block, keys_total), 0)
+    col_id = lax.broadcasted_iota(jnp.int32, (block, keys_total), 1)
     in_prompt = col_id - total
     prompt_slot = in_prompt // slot
     prompt_row = in_prompt - prompt_slot * slot
@@ -357,8 +357,11 @@
     far = jnp.int32(2**30)
     prompt_rank = jnp.where(prompt_row < prompt_rows, prompt_id, far)
     ahead = col_id - position
-    live_row = lax.broadcasted_iota(jnp.int32, (stacked, HEAD_DIM), 0)
-    live_position = mz * block + live_row - (live_row // block) * block
+    live_position = mz * block + lax.broadcasted_iota(jnp.int32, (block, HEAD_DIM), 0)
+
+    def per_head(rows_of_heads, factor, combine):
+        shape = rows_of_heads.shape
+        return combine(rows_of_heads.reshape(group, block, shape[1]), factor[None]).reshape(shape)
 
     wait_bytes(in_p.at[0 : (n - 1) * slot, :], sem_p)
     acc[...] = jnp.zeros_like(acc)
@@ -368,7 +371,8 @@
         length = len_ref[source]
         visible = seen_ref[source]
         allowed = jnp.where(col_id < total, ahead, prompt_rank - visible + 1) <= 0
-        live = live_position < length
+        bias = jnp.where(allowed, 0.0, NEG_FILL)
+        live = (live_position < length).astype(jnp.float32)
         for step in range(outer):
             @pl.when(step < mz)
             def _():
@@ -398,13 +402,13 @@
             ]
             query = jnp.concatenate([in_qg[stage, 0, :, c] for c in heads], axis=0)
             grad = jnp.concatenate([in_qg[stage, 1, :, c] for c in heads], axis=0)
-            grad_wide = jnp.where(live, grad.astype(jnp.float32), 0.0)
+            grad_wide = per_head(grad.astype(jnp.float32), live, jnp.multiply)
             grad = grad_wide.astype(jnp.bfloat16)
-            logits = jnp.where(allowed, dot_last(query, keys) * scale, NEG_FILL)
-            exped = jnp.exp(logits - jnp.max(logits, axis=1, keepdims=True))
+            logits = per_head(dot_last(query, keys) * (scale * LOG2E), bias, jnp.add)
+            exped = jnp.exp2(logits - jnp.max(logits, axis=1, keepdims=True))
             prob = exped * (1.0 / jnp.sum(exped, axis=1, keepdims=True))
             weights = prob.astype(jnp.bfloat16)
-            output = jnp.where(live, dot_plain(weights, values), 0.0).astype(jnp.bfloat16)
+            output = per_head(dot_plain(weights, values), live, jnp.multiply).astype(jnp.bfloat16)
             row_dot = jnp.sum(grad_wide * output.astype(jnp.float32), axis=1, keepdims=True)
             dlogit = (prob * (dot_last(grad, values) - row_dot)).astype(jnp.bfloat16)
             dquery = (dot_plain(dlogit, keys) * scale).astype(jnp.bfloat16)

time: 43.8 us -> 43.8 us (level)
  no operation moved by 1% of the time
where the time goes in v5:
time: 43.8 us; the launch traced here: 43.6 us
  Pallas kernels  43 us (98%)
  between operations  0.64 us (1%)
    pallas_call x1, Pallas kernels, kernel_body(): pl.pallas_call(functools.partial(kernel, n, inner, prompt_rows), out_shap...  40.7 us
    pallas_call x1, Pallas kernels, kernel_body(): pl.pallas_call(functools.partial(place_kernel, n), out_shape=shapes, in_s...  2.23 us

profile of v5, /device:TPU:0, one launch (start us, length us, event | category | flops | bytes accessed | tf_op | source)
XLA Modules:
  0.0 43.6 jit_solution(10118077854612029284)
XLA Ops:
  0.6 40.7 %shard_map.136 = (bf16[1,128,2048]{2,1,0:T(8,128)(2,1)}, bf16[8,16,2048]{2,1,0:T(8,128)(2,1)}, bf16[8,16,256]{2,1,0:T(8,128)(2,1)}, bf16[8,16,256]{2,1,0:T(8,128...) custom-call(bf16[8,16,2048]{2,1,0:T(8,128)(2,1)} %q_hbm.1, bf16[8,16,256]{2,1,0:T(8,128)(2,1)} %k_hbm.1, ...), custom_call_target="tpu_custom_call" | custom-call | tf_op jit(solution)/shard_map/pallas_call | solution.py:566
  41.4 2.2 %shard_map.137 = (bf16[1,128,2048]{2,1,0:T(8,128)(2,1)}, bf16[8,16,2048]{2,1,0:T(8,128)(2,1)}, bf16[8,16,256]{2,1,0:T(8,128)(2,1)}, bf16[8,16,256]{2,1,0:T(8,128...) custom-call(bf16[1,128,2048]{2,1,0:T(8,128)(2,1)} %get-tuple-element.12.refs_0_, ...), custom_call_target="tpu_custom_call" | custom-call | tf_op jit(solution)/shard_map/pallas_call | solution.py:602

commit v6 on v5

--- a/solution.py
+++ b/solution.py
@@ -329,10 +329,12 @@
              sem_send.at[1], sem_qg.at[unit], partner)
 
     units = outer * kv_heads
-    lead = 2
+    lead = 4
     send_keys(0)
     for step in range(1, n):
         send(send_p, in_p.at[tile(me, slot), :], sem_send.at[0], sem_p, lax.rem(me + step, n))
+    if outer > 1:
+        send_keys(1)
     loads[7].wait()
     loads[8].wait()
     for stage in range(outer):
@@ -381,8 +383,8 @@
             @pl.when(step == mz)
             def _():
                 wait_bytes(in_kv.at[stage, 0:rows, :], sem_kv.at[stage, step])
-        if stage + 1 < outer:
-            send_keys(stage + 1)
+        if stage + 2 < outer:
+            send_keys(stage + 2)
         for h in range(kv_heads):
             unit = stage * kv_heads + h
             cols = pl.ds(h * head_width, head_width)

time: 43.8 us -> 43.7 us (level)
  no operation moved by 1% of the time
where the time goes in v6:
time: 43.7 us; the launch traced here: 43.6 us
  Pallas kernels  42.9 us (98%)
  between operations  0.64 us (1%)
    pallas_call x1, Pallas kernels, kernel_body(): pl.pallas_call(functools.partial(kernel, n, inner, prompt_rows), out_shap...  40.7 us
    pallas_call x1, Pallas kernels, kernel_body(): pl.pallas_call(functools.partial(place_kernel, n), out_shape=shapes, in_s...  2.23 us

profile of v6, /device:TPU:0, one launch (start us, length us, event | category | flops | bytes accessed | tf_op | source)
XLA Modules:
  0.0 43.6 jit_solution(8715631842980630164)
XLA Ops:
  0.6 40.7 %shard_map.136 = (bf16[1,128,2048]{2,1,0:T(8,128)(2,1)}, bf16[8,16,2048]{2,1,0:T(8,128)(2,1)}, bf16[8,16,256]{2,1,0:T(8,128)(2,1)}, bf16[8,16,256]{2,1,0:T(8,128...) custom-call(bf16[8,16,2048]{2,1,0:T(8,128)(2,1)} %q_hbm.1, bf16[8,16,256]{2,1,0:T(8,128)(2,1)} %k_hbm.1, ...), custom_call_target="tpu_custom_call" | custom-call | tf_op jit(solution)/shard_map/pallas_call | solution.py:568
  41.4 2.2 %shard_map.137 = (bf16[1,128,2048]{2,1,0:T(8,128)(2,1)}, bf16[8,16,2048]{2,1,0:T(8,128)(2,1)}, bf16[8,16,256]{2,1,0:T(8,128)(2,1)}, bf16[8,16,256]{2,1,0:T(8,128...) custom-call(bf16[1,128,2048]{2,1,0:T(8,128)(2,1)} %get-tuple-element.12.refs_0_, ...), custom_call_target="tpu_custom_call" | custom-call | tf_op jit(solution)/shard_map/pallas_call | solution.py:604

commit v7 on v6

--- a/solution.py
+++ b/solution.py
@@ -424,6 +424,27 @@
                 grad_kv[stage, :, col : col + HEAD_DIM] = part[:total].astype(jnp.bfloat16)
                 acc[:, col : col + HEAD_DIM] += part[total:]
 
+            if h == kv_heads - 1:
+                for step in range(outer):
+                    @pl.when(mz - step >= 0)
+                    def _():
+                        for dx in range(inner):
+                            chunk = (mz - step) * inner + dx
+
+                            def go():
+                                send(grad_kv.at[stage, tile(chunk, rows), :], back_kv.at[mz, home],
+                                     sem_grad_out.at[step], sem_grad.at[mz], chunk)
+
+                            if step == 0:
+                                pl.when(mx != dx)(go)
+                            else:
+                                go()
+            if unit == units - 1:
+                grad_p[...] = acc[...].astype(jnp.bfloat16)
+                for step in range(1, n):
+                    peer = lax.rem(me + step, n)
+                    send(grad_p.at[tile(peer, slot), :], back_p.at[me], sem_send.at[4], sem_gp, peer)
+
             @pl.when(mz != stage)
             def _():
                 send(out_send.at[stage, :, cols], out_ref.at[0, tile(mz, block), cols],
@@ -441,25 +462,7 @@
                 grad_q.at[stage, tile(mx, rows), cols], back_q.at[home, :, cols], sem_local.at[1]
             ).start()
 
-        for step in range(outer):
-            @pl.when(mz - step >= 0)
-            def _():
-                for dx in range(inner):
-                    chunk = (mz - step) * inner + dx
-
-                    def go():
-                        send(grad_kv.at[stage, tile(chunk, rows), :], back_kv.at[mz, home],
-                             sem_grad_out.at[step], sem_grad.at[mz], chunk)
-
-                    if step == 0:
-                        pl.when(mx != dx)(go)
-                    else:
-                        go()
         back_kv[mz, home] = grad_kv[stage, own_rows, :]
-    grad_p[...] = acc[...].astype(jnp.bfloat16)
-    for step in range(1, n):
-        peer = lax.rem(me + step, n)
-        send(grad_p.at[tile(peer, slot), :], back_p.at[me], sem_send.at[4], sem_gp, peer)
     back_p[me] = grad_p[tile(me, slot), :]
 
     for step in range(outer):

time: 43.7 us -> 43.8 us (level)
  no operation moved by 1% of the time
where the time goes in v7:
time: 43.8 us; the launch traced here: 43.6 us
  Pallas kernels  43 us (98%)
  between operations  0.64 us (1%)
    pallas_call x1, Pallas kernels, kernel_body(): pl.pallas_call(functools.partial(kernel, n, inner, prompt_rows), out_shap...  40.8 us
    pallas_call x1, Pallas kernels, kernel_body(): pl.pallas_call(functools.partial(place_kernel, n), out_shape=shapes, in_s...  2.23 us

profile of v7, /device:TPU:0, one launch (start us, length us, event | category | flops | bytes accessed | tf_op | source)
XLA Modules:
  0.0 43.6 jit_solution(9713499599724887616)
XLA Ops:
  0.6 40.8 %shard_map.136 = (bf16[1,128,2048]{2,1,0:T(8,128)(2,1)}, bf16[8,16,2048]{2,1,0:T(8,128)(2,1)}, bf16[8,16,256]{2,1,0:T(8,128)(2,1)}, bf16[8,16,256]{2,1,0:T(8,128...) custom-call(bf16[8,16,2048]{2,1,0:T(8,128)(2,1)} %q_hbm.1, bf16[8,16,256]{2,1,0:T(8,128)(2,1)} %k_hbm.1, ...), custom_call_target="tpu_custom_call" | custom-call | tf_op jit(solution)/shard_map/pallas_call | solution.py:571
  41.4 2.2 %shard_map.137 = (bf16[1,128,2048]{2,1,0:T(8,128)(2,1)}, bf16[8,16,2048]{2,1,0:T(8,128)(2,1)}, bf16[8,16,256]{2,1,0:T(8,128)(2,1)}, bf16[8,16,256]{2,1,0:T(8,128...) custom-call(bf16[1,128,2048]{2,1,0:T(8,128)(2,1)} %get-tuple-element.12.refs_0_, ...), custom_call_target="tpu_custom_call" | custom-call | tf_op jit(solution)/shard_map/pallas_call | solution.py:607
